TPU v7x, 512 devices: a whole 4x8x8 slice. The times are simulated.
512 devices in a mesh: dp: 64 (over z, x, core), tensor: 8 (over y).
Axes of the slice: x: 4, y: 8, z: 8, core: 2. Of those that a mesh axis runs over, the one named last changes fastest.
Arguments:
- gradients: bfloat16 [16384, 14336], P('dp', 'tensor'), may hold values from -40 to 40
- errors: bfloat16 [16384, 14336], P('dp', 'tensor'), may hold values from -3 to 3
- warm_factor: bfloat16 [64, 14336], P(None, 'tensor'), may hold values from -5 to 5
Outputs:
- new_errors: bfloat16 [16384, 14336], P('dp', 'tensor')
- left_factor: float32 [64, 4096], P(None, 'dp')
- right_factor: bfloat16 [64, 14336], P(None, 'tensor')
All inputs are finite; a program needn't handle non-finite values.
Results may differ from a plain program's by a relative error of at most 0.0071.
Values may be sent and summed in bfloat16 or wider, within the bound.
A program may use at most 64 MiB of HBM per device.

v0:
```python
import jax
import jax.numpy as jnp
from jax import lax
from jax.sharding import PartitionSpec as P

ITERS = 2
REPLICAS = 4


def orthonormal(p_summed):
    gram_matrix = lax.dot_general(
        p_summed,
        p_summed,
        (((1,), (1,)), ((), ())),
        precision=lax.Precision.HIGHEST,
        preferred_element_type=jnp.float32,
    )
    lower_factor = jnp.linalg.cholesky(gram_matrix)
    return lax.linalg.triangular_solve(lower_factor, p_summed, left_side=True, lower=True)


def local(gradients, errors, warm_factor):
    corrected = (gradients.astype(jnp.float32) + errors.astype(jnp.float32)).astype(jnp.bfloat16)
    devices_dp = lax.axis_size("dp")
    group_size = devices_dp // REPLICAS
    row_dev = gradients.shape[0]
    full_rows = row_dev * group_size
    row_start = lax.axis_index("dp") % group_size * row_dev
    rank_size = warm_factor.shape[0]
    q_rounded = warm_factor
    p_own = None
    own_columns = None
    for iteration in range(ITERS):
        partial_value = lax.dot_general(
            q_rounded, corrected, (((1,), (1,)), ((), ())), preferred_element_type=jnp.float32
        )
        empty = jnp.zeros((rank_size, full_rows), jnp.float32)
        across = lax.psum(partial_value, "tensor")
        placed = lax.dynamic_update_slice_in_dim(empty, across, row_start, 1)
        p_summed = lax.psum(placed, "dp")
        left_whole = orthonormal(p_summed)
        p_whole = left_whole.astype(jnp.bfloat16)
        block_cols = full_rows // devices_dp
        own_columns = lax.dynamic_slice_in_dim(
            left_whole, lax.axis_index("dp") * block_cols, block_cols, 1
        )
        p_own = lax.dynamic_slice_in_dim(p_whole, row_start, row_dev, 1)
        local_right = jnp.dot(p_own, corrected, preferred_element_type=jnp.float32)
        q_summed = lax.psum(local_right, "dp")
        q_rounded = (q_summed / REPLICAS).astype(jnp.bfloat16)
    rebuilt = lax.dot_general(
        p_own, q_rounded, (((0,), (0,)), ((), ())), preferred_element_type=jnp.float32
    )
    new_errors = (gradients.astype(jnp.float32) + errors.astype(jnp.float32) - rebuilt).astype(
        jnp.bfloat16
    )
    return (new_errors, own_columns, q_rounded)


def solution(mesh):
    in_specs = (P("dp", "tensor"), P("dp", "tensor"), P(None, "tensor"))
    out_specs = (P("dp", "tensor"), P(None, "dp"), P(None, "tensor"))
    return jax.shard_map(local, mesh=mesh, in_specs=in_specs, out_specs=out_specs, check_vma=False)
```

profile of v0, /device:TPU:1, one launch (start us, length us, event | category | flops | bytes accessed | tf_op | source)
XLA Modules:
  0.0 987.8 jit_solution(5352646042755195644)
XLA Ops:
  7.2 1.7 fusion.1
  9.0 1.1 convolution_bitcast_fusion
  10.1 78.0 %all-reduce.7.cloned.1.call-done = f32[64,256]{1,0:T(8,128)} async-done(((f32[64,256]{1,0:T(8,128)}), f32[64,256]{1,0:T(8,128)}) %all-reduce.7.cloned.1.call-update) | async-done | bytes 65552 | tf_op jit(solution)/shard_map/psum | solution.py:38
  88.1 0.8 copy-done.9
  88.9 1.0 copy-done.4
  90.0 200.8 %all-reduce.9.cloned.1.call-done = f32[64,4096]{1,0:T(8,128)} async-done(((f32[64,4096]{1,0:T(8,128)}), f32[64,4096]{1,0:T(8,128)}) %all-reduce.9.cloned.1.call-update) | async-done | bytes 1048592 | tf_op jit(solution)/shard_map/psum | solution.py:40
  290.9 2.6 fusion.20
  293.5 0.1 copy.6
  293.6 5.8 cholesky.44
  299.5 0.6 compare_reduce_fusion.1
  300.1 0.7 fusion.4
  300.8 4.9 custom-call.6
  305.7 1.0 fusion.10
  306.7 1.1 fusion.6
  307.9 188.3 %all-reduce.11.cloned.1.call-done = f32[64,1792]{1,0:T(8,128)} async-done(((f32[64,1792]{1,0:T(8,128)}), f32[64,1792]{1,0:T(8,128)}) %all-reduce.11.cloned.1.call-update) | async-done | bytes 458768 | tf_op jit(solution)/shard_map/psum | solution.py:49
  496.1 2.1 fusion.2
  498.3 70.4 %all-reduce.13.cloned.1.call-done = f32[64,256]{1,0:T(8,128)} async-done(((f32[64,256]{1,0:T(8,128)}), f32[64,256]{1,0:T(8,128)}) %all-reduce.13.cloned.1.call-update) | async-done | bytes 65552 | tf_op jit(solution)/shard_map/psum | solution.py:38
  568.7 0.8 copy-done.10
  569.5 1.0 copy-done.3
  570.6 200.7 %all-reduce.15.cloned.1.call-done = f32[64,4096]{1,0:T(8,128)} async-done(((f32[64,4096]{1,0:T(8,128)}), f32[64,4096]{1,0:T(8,128)}) %all-reduce.15.cloned.1.call-update) | async-done | bytes 1048592 | tf_op jit(solution)/shard_map/psum | solution.py:40
  771.3 2.6 fusion.21
  774.0 5.8 cholesky.55
  779.9 0.6 compare_reduce_fusion
  780.5 0.7 fusion.5
  781.2 4.9 custom-call.7
  786.1 1.0 fusion.7
  787.2 1.0 copy-done.7
  788.2 1.1 fusion.15
  789.2 1.5 constant_dynamic-slice_fusion
  790.7 186.9 %all-reduce.17.cloned.1.call-done = f32[64,1792]{1,0:T(8,128)} async-done(((f32[64,1792]{1,0:T(8,128)}), f32[64,1792]{1,0:T(8,128)}) %all-reduce.17.cloned.1.call-update) | async-done | bytes 458768 | tf_op jit(solution)/shard_map/psum | solution.py:49
  977.6 1.0 multiply_convert_fusion
  978.7 2.3 fusion
  (38 shorter events, 0.7 us)
Async XLA Ops:
  7.2 1.8 copy-start
  7.2 80.9 %all-reduce.7.cloned.1.call-start = ((), (), s32[]{:S(2)}) async-start(), calls=%async_computation | async-start | bytes 131072 | tf_op jit(solution)/shard_map/psum | solution.py:38
  10.0 280.8 %all-reduce.9.cloned.1.call-start = ((), (), s32[]{:S(2)}) async-start(), calls=%async_computation.1 | async-start | bytes 2097152 | tf_op jit(solution)/shard_map/psum | solution.py:40
  88.1 0.8 copy-start.9
  88.9 1.0 copy-start.4
  90.0 406.2 %all-reduce.11.cloned.1.call-start = ((), (), s32[]{:S(2)}) async-start(), calls=%async_computation.2 | async-start | bytes 917504 | tf_op jit(solution)/shard_map/psum | solution.py:49
  290.9 14.8 %copy-start.1 = (f32[64,4096]{1,0:T(8,128)S(1)}, f32[64,4096]{1,0:T(8,128)}, u32[]{:S(2)}) copy-start(f32[64,4096]{1,0:T(8,128)} %all-reduce.9.cloned.1.call-done) | copy-start | bytes 3145732
  307.8 260.9 %all-reduce.13.cloned.1.call-start = ((), (), s32[]{:S(2)}) async-start(), calls=%async_computation.3 | async-start | bytes 131072 | tf_op jit(solution)/shard_map/psum | solution.py:38
  498.2 273.1 %all-reduce.15.cloned.1.call-start = ((), (), s32[]{:S(2)}) async-start(), calls=%async_computation.4 | async-start | bytes 2097152 | tf_op jit(solution)/shard_map/psum | solution.py:40
  568.7 0.8 copy-start.10
  569.5 1.0 copy-start.3
  570.6 407.0 %all-reduce.17.cloned.1.call-start = ((), (), s32[]{:S(2)}) async-start(), calls=%async_computation.5 | async-start | bytes 917504 | tf_op jit(solution)/shard_map/psum | solution.py:49
  771.3 14.8 %copy-start.2 = (f32[64,4096]{1,0:T(8,128)S(1)}, f32[64,4096]{1,0:T(8,128)}, u32[]{:S(2)}) copy-start(f32[64,4096]{1,0:T(8,128)} %all-reduce.15.cloned.1.call-done) | copy-start | bytes 3145732
  787.2 1.0 copy-start.7
  788.2 190.5 %copy-start.5 = (bf16[256,1792]{1,0:T(8,128)(2,1)S(1)}, bf16[256,1792]{1,0:T(8,128)(2,1)}, u32[]{:S(2)}) copy-start(bf16[256,1792]{1,0:T(8,128)(2,1)} %param.7) | copy-start | bytes 2752516
  788.2 190.5 %copy-start.6 = (bf16[256,1792]{1,0:T(8,128)(2,1)S(1)}, bf16[256,1792]{1,0:T(8,128)(2,1)}, u32[]{:S(2)}) copy-start(bf16[256,1792]{1,0:T(8,128)(2,1)} %param.6) | copy-start | bytes 2752516
  978.7 2.3 copy-start.8
Sparse Core Ops, SparseCore 0:
  10.9 77.1 all-reduce.6
  91.9 198.9 all-reduce.8
  307.9 188.1 all-reduce.10
  498.9 69.7 all-reduce.12
  572.3 198.9 all-reduce.14
  789.4 188.2 all-reduce.16
where the time goes:
time: 988 us
  waiting for transfers between devices  925 us (94%)
  other arithmetic  26.9 us (3%)
  matrix products  14.8 us (1%)
  between operations  14.3 us (1%)
    psum x2, waiting for transfers between devices, local(): p_summed = lax.psum(placed, 'dp')  402 us
    psum x2, waiting for transfers between devices, local(): q_summed = lax.psum(local_right, 'dp')  375 us
    psum x2, waiting for transfers between devices, local(): across = lax.psum(partial_value, 'tensor')  148 us
  transfers between devices with their start and end apart: 6, of which 6 were waited for; matrix products, arithmetic and copies ran while one was open for 0% of the time, Pallas kernels for 0%

commit v1 on v0

v1 whole, which is shorter than its diff:
```python
import functools

import jax
import jax.numpy as jnp
from jax import lax
from jax.experimental import pallas as pl
from jax.experimental.pallas import tpu as pltpu
from jax.sharding import PartitionSpec as P

ITERS = 2
MESH = pl.DeviceIdType.MESH
HIGH = lax.Precision.HIGHEST
F32 = jnp.float32
BF16 = jnp.bfloat16
RANK = 64


def lanes(shape):
    return lax.broadcasted_iota(jnp.int32, shape, 1)


def spread(x):
    low = lanes(x.shape) < RANK
    turned = pltpu.roll(x, RANK, 1)
    zero = jnp.zeros_like(x)
    first = jnp.concatenate([jnp.where(low, x, zero), jnp.where(low, turned, zero)], axis=0)
    second = jnp.concatenate([jnp.where(low, zero, turned), jnp.where(low, zero, x)], axis=0)
    return first, second


def split3(x):
    hi = x.astype(BF16)
    rest = x - hi.astype(F32)
    mid = rest.astype(BF16)
    return hi, mid, (rest - mid.astype(F32)).astype(BF16)


def nt(a, b):
    return lax.dot_general(a, b, (((1,), (1,)), ((), ())), precision=HIGH, preferred_element_type=F32)


def eliminate(rows, first, last, out_ref):
    block = 8
    for k0 in range(first, last, block):
        n = rows.shape[0]
        cols = [jnp.broadcast_to(rows[:, k0 + j : k0 + j + 1], (n, 128)) for j in range(block)]
        for i in range(block):
            pivot = cols[i][i : i + 1, :]
            row = rows[i : i + 1, :]
            out_ref[k0 + i : k0 + i + 1, :] = row * lax.rsqrt(pivot)
            if k0 + i == RANK - 1:
                break
            factor = cols[i] * (1.0 / pivot)
            rows = rows - factor * row
            for j in range(i + 1, block):
                cols[j] = cols[j] - factor * cols[j][i : i + 1, :]
        rows = rows[block:, :] if n > block else rows
    return rows


def kernel(
    geo, g_hbm, e_hbm, w_ref, ne_hbm, left_ref, right_ref,
    gv, ev, cv, ctv, nev,
    p_send, p_rs, p_z, p_ag, g_send, g_x, g_ag, chol,
    q_send, q_core, q_zs, q_z, q_xs, q_x, q_ag, l_send, l_recv,
    load_sem, store_sem,
    prs_s, prs_r, pz_s, pz_r, pag_s, pag_r, gx_s, gx_r, gag_s, gag_r,
    qc_s, qc_r, qz_s, qz_r, qx_s, qx_r, ax_s, ax_r, az_s, az_r, ac_s, ac_r, l_sem,
):
    nz, nx, nc, ny, owners = geo
    nb = nx * nc
    dp, y = lax.axis_index("dp"), lax.axis_index("tensor")
    c = lax.rem(dp, nc)
    b = lax.rem(dp, nb)
    x = lax.div(b, nc)
    z = lax.div(dp, nb)
    rows, cols = gv.shape
    half_rows, half = rows // 2, cols // 2

    def at(zz, bb, yy):
        return (zz * nb + bb, yy)

    def y_dev(j):
        return at(z, b, j)

    def z_dev(j):
        return at(j, b, y)

    def b_dev(j):
        return at(z, j, y)

    def x_dev(j):
        return at(z, j * nc + c, y)

    partner = at(z, x * nc + (1 - c), y)
    l_dst = nz * b + z
    l_src = lax.rem(dp, nz) * nb + lax.div(dp, nz)
    moved = l_dst != dp

    loads = [
        pltpu.make_async_copy(g_hbm, gv, load_sem.at[0]),
        pltpu.make_async_copy(e_hbm, ev, load_sem.at[1]),
    ]
    for load in loads:
        load.start()

    barrier = pltpu.get_barrier_semaphore()
    for n, me, dev in ((ny, y, y_dev), (nz, z, z_dev), (nb, b, b_dev)):
        for k in range(1, n):
            pl.semaphore_signal(barrier, inc=1, device_id=dev(lax.rem(me + k, n)), device_id_type=MESH)

    @pl.when(moved)
    def _():
        pl.semaphore_signal(barrier, inc=1, device_id=(l_dst, y), device_id_type=MESH)
        pl.semaphore_signal(barrier, inc=1, device_id=(l_src, y), device_id_type=MESH)

    def remote(src, dst, send, recv, dev):
        return pltpu.make_async_remote_copy(
            src_ref=src, dst_ref=dst, send_sem=send, recv_sem=recv, device_id=dev, device_id_type=MESH
        )

    def far_first(n):
        return sorted(range(1, n), key=lambda k: -min(k, n - k))

    def push(n, me, dev, src, dst, send, recv):
        for k in far_first(n):
            j = lax.rem(me + k, n)
            remote(src(j), dst, send.at[k], recv.at[me], dev(j)).start()

    def pull(n, me, dev, dst, send, recv):
        for k in far_first(n)[::-1]:
            j = lax.rem(me + k, n)
            remote(dst(j), dst(j), send.at[k], recv.at[j], dev(j)).wait_recv()

    def drain(n, me, dev, src, dst, send, recv):
        for k in range(1, n):
            j = lax.rem(me + k, n)
            remote(src(j), dst, send.at[k], recv.at[me], dev(j)).wait_send()

    pending = []

    def swap(n, me, dev, src, dst, send, recv):
        push(n, me, dev, src, dst(me), send, recv)
        pending.append(lambda: drain(n, me, dev, src, dst(me), send, recv))
        return lambda: pull(n, me, dev, dst, send, recv)

    q_packed = jnp.concatenate([w_ref[:, :half], w_ref[:, half:]], axis=0).T
    for load in loads:
        load.wait()
    cv[...] = (gv[...].astype(F32) + ev[...].astype(F32)).astype(BF16)

    for it in range(ITERS):
        last = it == ITERS - 1
        one = jnp.dot(cv[:, :half], q_packed, preferred_element_type=F32)
        two = jnp.dot(cv[:, half:], q_packed, preferred_element_type=F32)
        low = lanes((half_rows, 128)) < RANK
        packed = jnp.where(
            low,
            one[:half_rows] + pltpu.roll(two[:half_rows], RANK, 1),
            pltpu.roll(one[half_rows:], RANK, 1) + two[half_rows:],
        )
        p_send[it] = packed.reshape(ny, half_rows // ny, 128)
        if it == 0:
            pl.semaphore_wait(barrier, ny - 1 + nz - 1 + nb - 1 + jnp.where(moved, 2, 0))

        wait = swap(
            ny, y, y_dev, lambda j: p_send.at[it, j], lambda j: p_rs.at[it, j], prs_s.at[it], prs_r.at[it]
        )
        p_rs[it, y] = p_send[it, y]
        if it == 0:
            ctv[...] = cv[...].T.reshape(ctv.shape)
        wait()
        p_z[it, z] = functools.reduce(jnp.add, [p_rs[it, j] for j in range(ny)])
        wait = swap(nz, z, z_dev, lambda j: p_z.at[it, z], lambda j: p_z.at[it, j], pz_s.at[it], pz_r.at[it])
        wait()
        p_ag[it, y] = functools.reduce(jnp.add, [p_z[it, j] for j in range(nz)])
        wait = swap(ny, y, y_dev, lambda j: p_ag.at[it, y], lambda j: p_ag.at[it, j], pag_s.at[it], pag_r.at[it])
        wait()
        p_whole = p_ag[it].reshape(half_rows, 128)

        gram2 = lax.dot_general(
            p_whole, p_whole, (((0,), (0,)), ((), ())), precision=HIGH, preferred_element_type=F32
        )
        gram = gram2[:RANK] + pltpu.roll(gram2[RANK:], RANK, 1)
        g_send[it] = gram.reshape(g_send.shape[1:])
        g_x[it, b] = g_send[it, y]
        wait_gram = swap(nb, b, b_dev, lambda j: g_x.at[it, b], lambda j: g_x.at[it, j], gx_s.at[it], gx_r.at[it])

        first, second = spread(p_whole)
        terms = list(zip(split3(first), split3(second)))

        def right_term(core):
            total = None
            for one_p, two_p in terms:
                term = jnp.dot(ctv[0, core], one_p, preferred_element_type=F32)
                term += jnp.dot(ctv[1, core], two_p, preferred_element_type=F32)
                total = term if total is None else total + term
            return total

        q_send[it, 1 - c] = right_term(1 - c)
        half_copy = remote(q_send.at[it, 1 - c], q_core.at[it], qc_s.at[it], qc_r.at[it], partner)
        half_copy.start()
        pending.append(half_copy.wait_send)

        wait_gram()
        g_ag[it, y] = functools.reduce(jnp.add, [g_x[it, j] for j in range(nb)])
        wait_gram = swap(ny, y, y_dev, lambda j: g_ag.at[it, y], lambda j: g_ag.at[it, j], gag_s.at[it], gag_r.at[it])

        own_half = right_term(c)
        half_copy.wait_recv()
        q_zs[it] = (own_half + q_core[it]).reshape(q_zs.shape[1:])
        wait_z = swap(nz, z, z_dev, lambda j: q_zs.at[it, j], lambda j: q_z.at[it, j], qz_s.at[it], qz_r.at[it])

        wait_gram()
        gram = g_ag[it].reshape(RANK, 128)
        lane = lanes((RANK, 128))
        unit = (lane - RANK == lax.broadcasted_iota(jnp.int32, (RANK, 128), 0)).astype(F32)
        work = jnp.where(lane < RANK, gram, unit)
        work = eliminate(work, 0, RANK // 2, chol)

        wait_z()
        total = q_zs[it, z]
        for k in range(1, nz):
            total = total + q_z[it, lax.rem(z + k, nz)]
        q_xs[it] = total.reshape(q_xs.shape[1:])
        for k in far_first(nx):
            j = lax.rem(x + k, nx)

            @pl.when(j < owners)
            def _(k=k, j=j):
                remote(q_xs.at[it, j], q_x.at[it, x], qx_s.at[it, k], qx_r.at[it, x], x_dev(j)).start()

        eliminate(work, RANK // 2, RANK, chol)
        inverse = chol[...]
        turned = pltpu.roll(inverse, RANK, 1)
        solve = jnp.concatenate([jnp.where(lane < RANK, turned, 0.0), jnp.where(lane < RANK, 0.0, inverse)], axis=0)

        @pl.when(x < owners)
        def _():
            total = q_xs[it, x]
            for k in range(1, nx):
                j = lax.rem(x + k, nx)
                remote(q_x.at[it, j], q_x.at[it, j], qx_s.at[it, k], qx_r.at[it, j], x_dev(j)).wait_recv()
            for k in range(1, nx):
                total = total + q_x[it, lax.rem(x + k, nx)]
            mine = q_ag.at[it, c, z, x]
            mine[...] = (nt(total, solve) / nz).astype(BF16)
            for k in far_first(nx):
                remote(mine, mine, ax_s.at[it, k], ax_r.at[it, x], x_dev(lax.rem(x + k, nx))).start()

        if last:
            left = nt(p_whole, solve)
            turned_left = left.T
            per_half = nz // 2
            wide = rows // nz
            for zz in range(nz):
                h, o = zz // per_half, zz % per_half * wide
                l_send[zz] = turned_left[h * RANK : (h + 1) * RANK, o : o + wide]
            l_copy = remote(l_send.at[z], l_recv, l_sem.at[0], l_sem.at[1], (l_dst, y))

            @pl.when(moved)
            def _():
                l_copy.start()

            @pl.when(jnp.logical_not(moved))
            def _():
                l_recv[...] = l_send[z]

            p_first, p_second = spread(left)
            p_first, p_second = p_first.astype(BF16), p_second.astype(BF16)

        for k in range(1, nx):
            j = lax.rem(x + k, nx)

            @pl.when(j < owners)
            def _(k=k, j=j):
                slot = q_ag.at[it, c, z, j]
                remote(slot, slot, ax_s.at[it, k], ax_r.at[it, j], x_dev(j)).wait_recv()

        swap(nz, z, z_dev, lambda j: q_ag.at[it, c, z], lambda j: q_ag.at[it, c, j], az_s.at[it], az_r.at[it])()
        all_copy = remote(q_ag.at[it, c], q_ag.at[it, c], ac_s.at[it], ac_r.at[it], partner)
        all_copy.start()
        pending.append(all_copy.wait_send)
        other = q_ag.at[it, 1 - c]
        remote(other, other, ac_s.at[it], ac_r.at[it], partner).wait_recv()
        q_packed = q_ag[it].reshape(half, 128)

    q_turned = q_packed.T
    right_ref[:, :half] = q_turned[:RANK]
    right_ref[:, half:] = q_turned[RANK:]
    stores = []
    for at_half, left_half in ((0, p_first), (half, p_second)):
        span = slice(at_half, at_half + half)
        rebuilt = jnp.dot(left_half, q_turned, preferred_element_type=F32)
        nev[:, span] = (gv[:, span].astype(F32) + ev[:, span].astype(F32) - rebuilt).astype(BF16)
        stores.append(pltpu.make_async_copy(nev.at[:, span], ne_hbm.at[:, span], store_sem.at[len(stores)]))
        stores[-1].start()

    @pl.when(moved)
    def _():
        l_copy.wait()

    left_ref[...] = l_recv[...]
    for it in range(ITERS):
        for k in range(1, nx):
            j = lax.rem(x + k, nx)

            @pl.when(j < owners)
            def _(it=it, k=k, j=j):
                remote(q_xs.at[it, j], q_x.at[it, x], qx_s.at[it, k], qx_r.at[it, x], x_dev(j)).wait_send()

            @pl.when(x < owners)
            def _(it=it, k=k, j=j):
                mine = q_ag.at[it, c, z, x]
                remote(mine, mine, ax_s.at[it, k], ax_r.at[it, x], x_dev(j)).wait_send()

    for done in pending:
        done()
    for store in stores:
        store.wait()


def step(geo, gradients, errors, warm_factor):
    nz, nx, nc, ny, owners = geo
    nb = nx * nc
    rows, cols = gradients.shape
    half = cols // 2
    part = rows // 2 // ny
    core_rows = half // nc
    z_rows = core_rows // nz
    x_rows = z_rows // owners
    dma = pltpu.SemaphoreType.DMA
    vmem = pltpu.VMEM
    any_spec = pl.BlockSpec(memory_space=pl.ANY)
    vmem_spec = pl.BlockSpec(memory_space=pltpu.VMEM)
    return pl.pallas_call(
        functools.partial(kernel, geo),
        out_shape=(
            jax.ShapeDtypeStruct((rows, cols), BF16),
            jax.ShapeDtypeStruct((RANK, rows // nz), F32),
            jax.ShapeDtypeStruct((RANK, cols), BF16),
        ),
        in_specs=[any_spec, any_spec, vmem_spec],
        out_specs=(any_spec, vmem_spec, vmem_spec),
        scratch_shapes=[
            vmem((rows, cols), BF16), vmem((rows, cols), BF16), vmem((rows, cols), BF16),
            vmem((2, nc, core_rows, rows), BF16), vmem((rows, cols), BF16),
            vmem((ITERS, ny, part, 128), F32), vmem((ITERS, ny, part, 128), F32),
            vmem((ITERS, nz, part, 128), F32), vmem((ITERS, ny, part, 128), F32),
            vmem((ITERS, ny, RANK // ny, 128), F32), vmem((ITERS, nb, RANK // ny, 128), F32),
            vmem((ITERS, ny, RANK // ny, 128), F32), vmem((RANK, 128), F32),
            vmem((ITERS, nc, core_rows, 128), F32), vmem((ITERS, core_rows, 128), F32),
            vmem((ITERS, nz, z_rows, 128), F32), vmem((ITERS, nz, z_rows, 128), F32),
            vmem((ITERS, owners, x_rows, 128), F32), vmem((ITERS, nx, x_rows, 128), F32),
            vmem((ITERS, nc, nz, owners, x_rows, 128), BF16),
            vmem((nz, RANK, rows // nz), F32), vmem((RANK, rows // nz), F32),
            dma((2,)), dma((2,)),
            dma((ITERS, ny)), dma((ITERS, ny)), dma((ITERS, nz)), dma((ITERS, nz)), dma((ITERS, ny)), dma((ITERS, ny)),
            dma((ITERS, nb)), dma((ITERS, nb)), dma((ITERS, ny)), dma((ITERS, ny)),
            dma((ITERS,)), dma((ITERS,)), dma((ITERS, nz)), dma((ITERS, nz)), dma((ITERS, nx)), dma((ITERS, nx)),
            dma((ITERS, nx)), dma((ITERS, nx)), dma((ITERS, nz)), dma((ITERS, nz)), dma((ITERS,)), dma((ITERS,)),
            dma((2,)),
        ],
        compiler_params=pltpu.CompilerParams(
            collective_id=0, has_side_effects=True, vmem_limit_bytes=40 * 1024 * 1024
        ),
        name="power_step",
    )(gradients, errors, warm_factor)


def build(mesh, geo):
    in_specs = (P("dp", "tensor"), P("dp", "tensor"), P(None, "tensor"))
    out_specs = (P("dp", "tensor"), P(None, "dp"), P(None, "tensor"))
    return jax.shard_map(
        functools.partial(step, geo), mesh=mesh, in_specs=in_specs, out_specs=out_specs, check_vma=False
    )


def solution(mesh):
    return build(mesh, (4, 8, 2, 8, 7))
```

time: 988 us -> 107 us (0.11)
  waiting for transfers between devices: 925 us -> 0 us
  Pallas kernels: 0 us -> 101 us
  other arithmetic: 26.9 us -> 0 us
  matrix products: 14.8 us -> 0 us
  between operations: 14.3 us -> 0.65 us
    psum x6 -> x0, waiting for transfers between devices: 925 us -> none  [the longest x2 402 us: local(): p_summed = lax.psum(placed, 'dp')]
    pallas_call x0 -> x1, Pallas kernels: none -> 101 us  [step(): pl.pallas_call(functools.partial(kernel, geo), out_shape=(jax.ShapeDtypeS...]
    another operation x10 -> x0, other arithmetic: 24.1 us -> none  [the longest x6 13 us: orthonormal(): lower_factor = jnp.linalg.cholesky(gram_matrix)]
    dot_general x7 -> x0, matrix products: 12.7 us -> none  [the longest x2 5.21 us: orthonormal(): lax.dot_general(p_summed, p_summed, (((1,), (1,)), ((), ())), precision=l...]
  transfers between devices with their start and end apart: 6 -> 0, of which waited for: 6 -> 0; matrix products, arithmetic and copies ran while one was open for 0% -> 0% of each run, Pallas kernels for 0% -> 0%
where the time goes in v1:
time: 107 us
  Pallas kernels  101 us (94%)
  local copies, waits for them, and re-layouts  5.52 us (5%)
    pallas_call x1, Pallas kernels, step(): pl.pallas_call(functools.partial(kernel, geo), out_shape=(jax.ShapeDtypeS...  101 us
    unnamed x9, local copies, waits for them, and re-layouts  5.52 us

profile of v1, /device:TPU:1, one launch (start us, length us, event | category | flops | bytes accessed | tf_op | source)
XLA Modules:
  0.0 106.7 jit_solution(9707817213426788913)
XLA Ops:
  0.6 0.0 copy-start
  0.6 1.2 %copy-done = bf16[256,1792]{1,0:T(8,128)(2,1)S(1)} copy-done((bf16[256,1792]{1,0:T(8,128)(2,1)S(1)}, bf16[256,1792]{1,0:T(8,128)(2,1)}, u32[]{:S(2)}) %copy-start) | copy-done | bytes 917528
  1.8 0.0 copy-start.1
  1.8 1.2 %copy-done.1 = bf16[256,1792]{1,0:T(8,128)(2,1)S(1)} copy-done((bf16[256,1792]{1,0:T(8,128)(2,1)S(1)}, bf16[256,1792]{1,0:T(8,128)(2,1)}, u32[]{:S(2)}) %copy-start.1) | copy-done | bytes 917528
  3.0 0.0 copy-start.2
  3.0 0.9 copy-done.2
  3.9 100.6 %power_step.1 = (bf16[256,1792]{1,0:T(8,128)(2,1)S(1)}, f32[64,64]{1,0:T(8,128)S(1)}, bf16[64,1792]{1,0:T(8,128)(2,1)S(1)}) custom-call(bf16[256,1792]{1,0:T(8,128)(2,1)S(1)} %copy-done, bf16[256,1792]{1,0:T(8,128)(2,1)S(1)} %copy-done.1, bf16[64,1792]{1,0:T(8,128)(2,1)S(1)} %copy-done.2), custom_call_target="tpu_custom_call" | custom-call | tf_op jit(solution)/shard_map/power_step/pallas_call | solution.py:336
  104.5 0.9 copy.9
  105.4 0.6 copy.10
  106.0 0.7 copy.11
Async XLA Ops:
  0.6 1.2 %copy-start = (bf16[256,1792]{1,0:T(8,128)(2,1)S(1)}, bf16[256,1792]{1,0:T(8,128)(2,1)}, u32[]{:S(2)}) copy-start(bf16[256,1792]{1,0:T(8,128)(2,1)} %g_hbm.1) | copy-start | bytes 2752516
  1.8 1.2 %copy-start.1 = (bf16[256,1792]{1,0:T(8,128)(2,1)S(1)}, bf16[256,1792]{1,0:T(8,128)(2,1)}, u32[]{:S(2)}) copy-start(bf16[256,1792]{1,0:T(8,128)(2,1)} %e_hbm.1) | copy-start | bytes 2752516
  3.0 0.9 copy-start.2

commit v2 on v1

v2 whole, which is shorter than its diff:
```python
import functools

import jax
import jax.numpy as jnp
from jax import lax
from jax.experimental import pallas as pl
from jax.experimental.pallas import tpu as pltpu
from jax.sharding import PartitionSpec as P

ITERS = 2
MESH = pl.DeviceIdType.MESH
HIGH = lax.Precision.HIGHEST
F32 = jnp.float32
BF16 = jnp.bfloat16
RANK = 64
TILE = 16


def lanes(shape):
    return lax.broadcasted_iota(jnp.int32, shape, 1)


def spread(x):
    low = lanes(x.shape) < RANK
    turned = pltpu.roll(x, RANK, 1)
    zero = jnp.zeros_like(x)
    first = jnp.concatenate([jnp.where(low, x, zero), jnp.where(low, turned, zero)], axis=0)
    second = jnp.concatenate([jnp.where(low, zero, turned), jnp.where(low, zero, x)], axis=0)
    return first, second


def split3(x):
    hi = x.astype(BF16)
    rest = x - hi.astype(F32)
    mid = rest.astype(BF16)
    return hi, mid, (rest - mid.astype(F32)).astype(BF16)


def nt(a, b):
    return lax.dot_general(a, b, (((1,), (1,)), ((), ())), precision=HIGH, preferred_element_type=F32)


def eliminate(rows, out_ref):
    block = 8
    for k0 in range(0, RANK, block):
        n = rows.shape[0]
        cols = [jnp.broadcast_to(rows[:, k0 + j : k0 + j + 1], (n, 128)) for j in range(block)]
        for i in range(block):
            pivot = cols[i][i : i + 1, :]
            row = rows[i : i + 1, :]
            out_ref[k0 + i : k0 + i + 1, :] = row * lax.rsqrt(pivot)
            if k0 + i == RANK - 1:
                break
            factor = cols[i] * (1.0 / pivot)
            rows = rows - factor * row
            for j in range(i + 1, block):
                cols[j] = cols[j] - factor * cols[j][i : i + 1, :]
        rows = rows[block:, :] if n > block else rows


def kernel(
    geo, g_hbm, e_hbm, w_hbm, ne_hbm, left_ref, right_ref,
    gv, ev, wv, cv, ctv, nev,
    p_send, p_rs, p_z, p_ag, g_send, g_x, g_ag, chol,
    q_send, q_core, q_sum, q_x, q_ag, size_ref, l_send, l_recv,
    load_sem, store_sem, send_sem, recv_sem,
):
    nrep, nzl, nx, nc, ny = geo
    nb = nzl * nx * nc
    nz = nrep * nzl
    chips = nz * nx
    owners = q_ag.shape[2]
    dp, y = lax.axis_index("dp"), lax.axis_index("tensor")
    c = lax.rem(dp, nc)
    b = lax.rem(dp, nb)
    rep = lax.div(dp, nb)
    chip = lax.div(dp, nc)
    x = lax.rem(chip, nx)
    z = lax.div(chip, nx)
    rows, cols = gv.shape
    half_rows, half = rows // 2, cols // 2
    partner = (dp + 1 - 2 * c, y)
    l_dst = nrep * b + rep
    l_src = lax.rem(dp, nrep) * nb + lax.div(dp, nrep)
    moved = l_dst != dp

    loads = [
        pltpu.make_async_copy(src, dst, load_sem.at[i])
        for i, (src, dst) in enumerate(((w_hbm, wv), (g_hbm, gv), (e_hbm, ev)))
    ]
    for load in loads:
        load.start()

    def y_peers(act):
        for k in sorted(range(1, ny), key=lambda k: -min(k, ny - k)):
            j = lax.rem(y + k, ny)
            act(j, (dp, j))

    def rep_peers(act):
        for k in sorted(range(1, nrep), key=lambda k: -min(k, nrep - k)):
            j = lax.rem(rep + k, nrep)
            act(j, (j * nb + b, y))

    def block_peers(act):
        for k in range(1, nb):
            j = lax.rem(b + k, nb)
            act(j, (rep * nb + j, y))

    def chip_peers(act):
        def at_z(i, carry):
            step = lax.div(i + 1, 2)
            to_z = lax.rem(z + nz // 2 + jnp.where(lax.rem(i, 2) == 1, nz - step, step), nz)
            for k in sorted(range(nx), key=lambda k: -min(k, nx - k)):
                j = to_z * nx + lax.rem(x + k, nx)
                if k == 0:
                    pl.when(j != chip)(functools.partial(act, j, (j * nc + c, y)))
                else:
                    act(j, (j * nc + c, y))
            return carry

        lax.fori_loop(0, nz, at_z, 0)

    barrier = pltpu.get_barrier_semaphore()

    def greet(device):
        pl.semaphore_signal(barrier, inc=1, device_id=device, device_id_type=MESH)

    chip_peers(lambda j, device: greet(device))
    y_peers(lambda j, device: greet(device))
    for k in range(nzl * nx):
        greet((rep * nb + lax.rem(b + nc * k, nb) + 1 - 2 * c, y))

    @pl.when(moved)
    def _():
        greet((l_dst, y))
        greet((l_src, y))

    greeted = chips - 1 + ny - 1 + nzl * nx

    def remote(src, dst, stage, it, device):
        return pltpu.make_async_remote_copy(
            src_ref=src, dst_ref=dst, send_sem=send_sem.at[stage, it], recv_sem=recv_sem.at[stage, it],
            device_id=device, device_id_type=MESH,
        )

    pending = []

    def swap(stage, it, peers, src, slots, me, count):
        peers(lambda j, device: remote(src(j), slots.at[me], stage, it, device).start())
        whole = remote(slots.at[:count], slots.at[:count], stage, it, partner)
        pending.append(whole.wait_send)
        return whole.wait_recv

    def total(slots, n):
        return functools.reduce(jnp.add, [slots[j] for j in range(n)])

    loads[0].wait()
    q_packed = jnp.concatenate([wv[:, :half], wv[:, half:]], axis=0).T
    loads[1].wait()
    loads[2].wait()
    cv[...] = (gv[...].astype(F32) + ev[...].astype(F32)).astype(BF16)
    low = lanes((half_rows, 128)) < RANK

    for it in range(ITERS):
        one = jnp.dot(cv[:, :half], q_packed, preferred_element_type=F32)
        two = jnp.dot(cv[:, half:], q_packed, preferred_element_type=F32)
        packed = jnp.where(
            low,
            one[:half_rows] + pltpu.roll(two[:half_rows], RANK, 1),
            pltpu.roll(one[half_rows:], RANK, 1) + two[half_rows:],
        )
        p_send[it] = packed.reshape(ny, half_rows // ny, 128)
        if it == 0:
            pl.semaphore_wait(barrier, greeted + jnp.where(moved, 2, 0))
        wait = swap(0, it, y_peers, lambda j: p_send.at[it, j], p_rs.at[it], y, ny - 1)
        p_rs[it, y] = p_send[it, y]
        if it == 0:
            ctv[...] = cv[...].T.reshape(ctv.shape)
        wait()
        p_z[it, rep] = total(p_rs.at[it], ny)
        swap(1, it, rep_peers, lambda j: p_z.at[it, rep], p_z.at[it], rep, nrep - 1)()
        p_ag[it, y] = total(p_z.at[it], nrep)
        swap(2, it, y_peers, lambda j: p_ag.at[it, y], p_ag.at[it], y, ny - 1)()
        p_whole = p_ag[it].reshape(half_rows, 128)

        first, second = spread(p_whole)
        terms = list(zip(split3(first), split3(second)))

        def right_term(core):
            result = None
            for one_p, two_p in terms:
                term = jnp.dot(ctv[0, core], one_p, preferred_element_type=F32)
                term += jnp.dot(ctv[1, core], two_p, preferred_element_type=F32)
                result = term if result is None else result + term
            return result

        q_send[it] = right_term(1 - c)
        half_copy = remote(q_send.at[it], q_core.at[it], 3, it, partner)
        half_copy.start()
        pending.append(half_copy.wait_send)

        gram2 = lax.dot_general(
            p_whole, p_whole, (((0,), (0,)), ((), ())), precision=HIGH, preferred_element_type=F32
        )
        gram = gram2[:RANK] + pltpu.roll(gram2[RANK:], RANK, 1)
        low_t = lanes((TILE, 128)) < RANK
        for h in range(nc):
            upper, lower = gram[2 * h * TILE : (2 * h + 1) * TILE], gram[(2 * h + 1) * TILE : (2 * h + 2) * TILE]
            g_send[it, h] = jnp.where(low_t, upper, pltpu.roll(lower, RANK, 1))
        g_x[it, b] = g_send[it, c]
        wait_gram = swap(4, it, block_peers, lambda j: g_send.at[it, lax.rem(j, nc)], g_x.at[it], b, nb - 1)

        own_half = right_term(c)
        half_copy.wait_recv()
        q_sum[it] = (own_half + q_core[it]).reshape(q_sum.shape[1:])

        def send_share(j, device):
            @pl.when(j < owners)
            def _():
                remote(q_sum.at[it, j], q_x.at[it, chip], 5, it, device).start()

        chip_peers(send_share)

        wait_gram()
        g_ag[it, c] = total(g_x.at[it], nb)
        own_gram, other_gram = g_ag.at[it, c], g_ag.at[it, 1 - c]
        gram_copy = remote(own_gram, own_gram, 6, it, partner)
        gram_copy.start()
        pending.append(gram_copy.wait_send)
        remote(other_gram, other_gram, 6, it, partner).wait_recv()
        pieces = []
        for h in range(nc):
            whole = g_ag[it, h]
            pieces += [whole, pltpu.roll(whole, RANK, 1)]
        lane = lanes((RANK, 128))
        unit = (lane - RANK == lax.broadcasted_iota(jnp.int32, (RANK, 128), 0)).astype(F32)
        eliminate(jnp.where(lane < RANK, jnp.concatenate(pieces, axis=0), unit), chol)
        inverse = chol[...]
        turned = pltpu.roll(inverse, RANK, 1)
        solve = jnp.concatenate([jnp.where(lane < RANK, turned, 0.0), jnp.where(lane < RANK, 0.0, inverse)], axis=0)

        @pl.when(chip < owners)
        def _():
            q_x[it, chip] = q_sum[it, chip]
            most = q_x.at[it, : chips - 1]
            remote(most, most, 5, it, partner).wait_recv()
            mine = q_ag.at[it, c, chip]
            mine[...] = (nt(jnp.sum(q_x[it], axis=0), solve) / nrep).astype(BF16)
            chip_peers(lambda j, device: remote(mine, mine, 7, it, device).start())

        if it == ITERS - 1:
            left = nt(p_whole, solve)
            turned_left = left.T
            per_half = nrep // 2
            wide = rows // nrep
            for r in range(nrep):
                h, o = r // per_half, r % per_half * wide
                l_send[r] = turned_left[h * RANK : (h + 1) * RANK, o : o + wide]
            l_copy = remote(l_send.at[rep], l_recv, 9, 0, (l_dst, y))

            @pl.when(moved)
            def _():
                l_copy.start()

            @pl.when(jnp.logical_not(moved))
            def _():
                l_recv[...] = l_send[rep]

            p_first, p_second = spread(left)
            p_first, p_second = p_first.astype(BF16), p_second.astype(BF16)

        @pl.when(chip < owners)
        def _():
            others = q_ag.at[it, c, : owners - 1]
            remote(others, others, 7, it, partner).wait_recv()

        @pl.when(chip >= owners)
        def _():
            others = q_ag.at[it, c]
            remote(others, others, 7, it, partner).wait_recv()

        all_copy = remote(q_ag.at[it, c], q_ag.at[it, c], 8, it, partner)
        all_copy.start()
        pending.append(all_copy.wait_send)
        other = q_ag.at[it, 1 - c]
        remote(other, other, 8, it, partner).wait_recv()
        q_packed = q_ag[it].reshape(half, 128)

    q_turned = q_packed.T
    right_ref[:, :half] = q_turned[:RANK]
    right_ref[:, half:] = q_turned[RANK:]
    stores = []
    for at_half, left_half in ((0, p_first), (half, p_second)):
        span = slice(at_half, at_half + half)
        rebuilt = jnp.dot(left_half, q_turned, preferred_element_type=F32)
        nev[:, span] = (gv[:, span].astype(F32) + ev[:, span].astype(F32) - rebuilt).astype(BF16)
        stores.append(pltpu.make_async_copy(nev.at[:, span], ne_hbm.at[:, span], store_sem.at[len(stores)]))
        stores[-1].start()

    @pl.when(moved)
    def _():
        l_copy.wait()

    left_ref[...] = l_recv[...]
    sized = size_ref.at[: chips - 1]
    for it in range(ITERS):

        @pl.when(chip < owners)
        def _():
            most = q_sum.at[it, : owners - 1]
            remote(most, most, 5, it, partner).wait_send()
            remote(sized, sized, 7, it, partner).wait_send()

        @pl.when(chip >= owners)
        def _():
            remote(q_sum.at[it], q_sum.at[it], 5, it, partner).wait_send()

    for done in pending:
        done()
    for store in stores:
        store.wait()


def step(geo, gradients, errors, warm_factor):
    nrep, nzl, nx, nc, ny = geo
    nb = nzl * nx * nc
    chips = nrep * nzl * nx
    rows, cols = gradients.shape
    half = cols // 2
    part = rows // 2 // ny
    core_rows = half // nc
    owners = core_rows // TILE
    stages = 10
    dma = pltpu.SemaphoreType.DMA
    vmem = pltpu.VMEM
    any_spec = pl.BlockSpec(memory_space=pl.ANY)
    vmem_spec = pl.BlockSpec(memory_space=pltpu.VMEM)
    return pl.pallas_call(
        functools.partial(kernel, geo),
        out_shape=(
            jax.ShapeDtypeStruct((rows, cols), BF16),
            jax.ShapeDtypeStruct((RANK, rows // nrep), F32),
            jax.ShapeDtypeStruct((RANK, cols), BF16),
        ),
        in_specs=[any_spec, any_spec, any_spec],
        out_specs=(any_spec, vmem_spec, vmem_spec),
        scratch_shapes=[
            vmem((rows, cols), BF16), vmem((rows, cols), BF16), vmem((RANK, cols), BF16), vmem((rows, cols), BF16),
            vmem((2, nc, core_rows, rows), BF16), vmem((rows, cols), BF16),
            vmem((ITERS, ny, part, 128), F32), vmem((ITERS, ny, part, 128), F32),
            vmem((ITERS, nrep, part, 128), F32), vmem((ITERS, ny, part, 128), F32),
            vmem((ITERS, nc, TILE, 128), F32), vmem((ITERS, nb, TILE, 128), F32),
            vmem((ITERS, nc, TILE, 128), F32), vmem((RANK, 128), F32),
            vmem((ITERS, core_rows, 128), F32), vmem((ITERS, core_rows, 128), F32),
            vmem((ITERS, owners, TILE, 128), F32), vmem((ITERS, chips, TILE, 128), F32),
            vmem((ITERS, nc, owners, TILE, 128), BF16), vmem((chips, TILE, 128), BF16),
            vmem((nrep, RANK, rows // nrep), F32), vmem((RANK, rows // nrep), F32),
            dma((3,)), dma((2,)), dma((stages, ITERS)), dma((stages, ITERS)),
        ],
        compiler_params=pltpu.CompilerParams(
            collective_id=0, has_side_effects=True, vmem_limit_bytes=60 * 1024 * 1024
        ),
        name="power_step",
    )(gradients, errors, warm_factor)


def build(mesh, geo):
    in_specs = (P("dp", "tensor"), P("dp", "tensor"), P(None, "tensor"))
    out_specs = (P("dp", "tensor"), P(None, "dp"), P(None, "tensor"))
    return jax.shard_map(
        functools.partial(step, geo), mesh=mesh, in_specs=in_specs, out_specs=out_specs, check_vma=False
    )


def solution(mesh):
    return build(mesh, (4, 2, 4, 2, 8))
```

time: 107 us -> 88.4 us (0.83)
  Pallas kernels: 101 us -> 84.1 us
  local copies, waits for them, and re-layouts: 5.52 us -> 3.51 us
    pallas_call x1, Pallas kernels: 101 us -> 84.1 us  [step(): pl.pallas_call(functools.partial(kernel, geo), out_shape=(jax.ShapeDtypeS...]
    unnamed x9 -> x7, local copies, waits for them, and re-layouts: 5.52 us -> 3.51 us
where the time goes in v2:
time: 88.4 us; the launch traced here: 88.2 us
  Pallas kernels  84.1 us (95%)
  local copies, waits for them, and re-layouts  3.51 us (4%)
    pallas_call x1, Pallas kernels, step(): pl.pallas_call(functools.partial(kernel, geo), out_shape=(jax.ShapeDtypeS...  84.1 us
    unnamed x7, local copies, waits for them, and re-layouts  3.51 us

profile of v2, /device:TPU:1, one launch (start us, length us, event | category | flops | bytes accessed | tf_op | source)
XLA Modules:
  0.0 88.2 jit_solution(13357144932457095260)
XLA Ops:
  0.6 84.1 %power_step.1 = (bf16[256,1792]{1,0:T(8,128)(2,1)}, f32[64,64]{1,0:T(8,128)}, bf16[64,1792]{1,0:T(8,128)(2,1)}) custom-call(bf16[256,1792]{1,0:T(8,128)(2,1)} %g_hbm.1, bf16[256,1792]{1,0:T(8,128)(2,1)} %e_hbm.1, bf16[64,1792]{1,0:T(8,128)(2,1)} %w_hbm.1), custom_call_target="tpu_custom_call" | custom-call | tf_op jit(solution)/shard_map/power_step/pallas_call | solution.py:338
  84.7 0.0 copy-start.1
  84.7 0.0 copy-start
  84.7 2.2 %copy.9 = bf16[256,1792]{1,0:T(8,128)(2,1)} copy(bf16[256,1792]{1,0:T(8,128)(2,1)} %get-tuple-element.6) | data formatting | bytes 1835008
  86.9 0.0 copy-done.1
  86.9 0.6 copy.10
  87.5 0.0 copy-done
  87.5 0.7 copy.11
Async XLA Ops:
  84.7 2.2 %copy-start.1 = (f32[64,64]{1,0:T(8,128)S(1)}, f32[64,64]{1,0:T(8,128)}, u32[]{:S(2)}) copy-start(f32[64,64]{1,0:T(8,128)} %get-tuple-element.7) | copy-start | bytes 49156
  84.7 2.8 %copy-start = (bf16[64,1792]{1,0:T(8,128)(2,1)S(1)}, bf16[64,1792]{1,0:T(8,128)(2,1)}, u32[]{:S(2)}) copy-start(bf16[64,1792]{1,0:T(8,128)(2,1)} %get-tuple-element.8) | copy-start | bytes 688132

commit v3 on v2

--- a/solution.py
+++ b/solution.py
@@ -29,11 +29,9 @@
     return first, second
 
 
-def split3(x):
+def split2(x):
     hi = x.astype(BF16)
-    rest = x - hi.astype(F32)
-    mid = rest.astype(BF16)
-    return hi, mid, (rest - mid.astype(F32)).astype(BF16)
+    return hi, (x - hi.astype(F32)).astype(BF16)
 
 
 def nt(a, b):
@@ -59,17 +57,18 @@
 
 
 def kernel(
-    geo, g_hbm, e_hbm, w_hbm, ne_hbm, left_ref, right_ref,
-    gv, ev, wv, cv, ctv, nev,
+    geo, g_hbm, e_hbm, w_hbm, ne_out, left_out, right_out,
+    gv, ev, wv, cv, ctv, nev, rv,
     p_send, p_rs, p_z, p_ag, g_send, g_x, g_ag, chol,
     q_send, q_core, q_sum, q_x, q_ag, size_ref, l_send, l_recv,
-    load_sem, store_sem, send_sem, recv_sem,
+    load_sem, store_sem, send_sem, recv_sem, piece_send, piece_recv,
 ):
     nrep, nzl, nx, nc, ny = geo
     nb = nzl * nx * nc
     nz = nrep * nzl
     chips = nz * nx
     owners = q_ag.shape[2]
+    share = owners // nrep
     dp, y = lax.axis_index("dp"), lax.axis_index("tensor")
     c = lax.rem(dp, nc)
     b = lax.rem(dp, nb)
@@ -77,6 +76,9 @@
     chip = lax.div(dp, nc)
     x = lax.rem(chip, nx)
     z = lax.div(chip, nx)
+    at_rep = lax.div(b, nc)
+    owns = at_rep < share
+    mine_at = rep * share + at_rep
     rows, cols = gv.shape
     half_rows, half = rows // 2, cols // 2
     partner = (dp + 1 - 2 * c, y)
@@ -84,10 +86,9 @@
     l_src = lax.rem(dp, nrep) * nb + lax.div(dp, nrep)
     moved = l_dst != dp
 
-    loads = [
-        pltpu.make_async_copy(src, dst, load_sem.at[i])
-        for i, (src, dst) in enumerate(((w_hbm, wv), (g_hbm, gv), (e_hbm, ev)))
-    ]
+    parts = [pl.ds(h * half_rows, half_rows) for h in range(2)]
+    pairs = [(w_hbm, wv)] + [(src.at[part], dst.at[part]) for part in parts for src, dst in ((g_hbm, gv), (e_hbm, ev))]
+    loads = [pltpu.make_async_copy(src, dst, load_sem.at[i]) for i, (src, dst) in enumerate(pairs)]
     for load in loads:
         load.start()
 
@@ -156,19 +157,18 @@
 
     loads[0].wait()
     q_packed = jnp.concatenate([wv[:, :half], wv[:, half:]], axis=0).T
-    loads[1].wait()
-    loads[2].wait()
-    cv[...] = (gv[...].astype(F32) + ev[...].astype(F32)).astype(BF16)
     low = lanes((half_rows, 128)) < RANK
 
     for it in range(ITERS):
-        one = jnp.dot(cv[:, :half], q_packed, preferred_element_type=F32)
-        two = jnp.dot(cv[:, half:], q_packed, preferred_element_type=F32)
-        packed = jnp.where(
-            low,
-            one[:half_rows] + pltpu.roll(two[:half_rows], RANK, 1),
-            pltpu.roll(one[half_rows:], RANK, 1) + two[half_rows:],
-        )
+        ones, twos = [], []
+        for h, part in enumerate(parts):
+            if it == 0:
+                loads[1 + 2 * h].wait()
+                loads[2 + 2 * h].wait()
+                cv[part] = (gv[part].astype(F32) + ev[part].astype(F32)).astype(BF16)
+            ones.append(jnp.dot(cv[part, :half], q_packed, preferred_element_type=F32))
+            twos.append(jnp.dot(cv[part, half:], q_packed, preferred_element_type=F32))
+        packed = jnp.where(low, ones[0] + pltpu.roll(twos[0], RANK, 1), pltpu.roll(ones[1], RANK, 1) + twos[1])
         p_send[it] = packed.reshape(ny, half_rows // ny, 128)
         if it == 0:
             pl.semaphore_wait(barrier, greeted + jnp.where(moved, 2, 0))
@@ -184,20 +184,28 @@
         p_whole = p_ag[it].reshape(half_rows, 128)
 
         first, second = spread(p_whole)
-        terms = list(zip(split3(first), split3(second)))
-
-        def right_term(core):
+        terms = list(zip(split2(first), split2(second)))
+
+        def right_term(core, group):
             result = None
             for one_p, two_p in terms:
-                term = jnp.dot(ctv[0, core], one_p, preferred_element_type=F32)
-                term += jnp.dot(ctv[1, core], two_p, preferred_element_type=F32)
+                term = jnp.dot(ctv[0, core, group], one_p, preferred_element_type=F32)
+                term += jnp.dot(ctv[1, core, group], two_p, preferred_element_type=F32)
                 result = term if result is None else result + term
             return result
 
-        q_send[it] = right_term(1 - c)
-        half_copy = remote(q_send.at[it], q_core.at[it], 3, it, partner)
-        half_copy.start()
-        pending.append(half_copy.wait_send)
+        groups = [lax.rem(rep + k, nrep) for k in sorted(range(nrep), key=lambda k: -min(k, nrep - k))]
+        pieces = []
+        for i, group in enumerate(groups):
+            q_send[it, i] = right_term(1 - c, group)
+            pieces.append(
+                pltpu.make_async_remote_copy(
+                    src_ref=q_send.at[it, i], dst_ref=q_core.at[it, i], send_sem=piece_send.at[it, i],
+                    recv_sem=piece_recv.at[it, i], device_id=partner, device_id_type=MESH,
+                )
+            )
+            pieces[-1].start()
+            pending.append(pieces[-1].wait_send)
 
         gram2 = lax.dot_general(
             p_whole, p_whole, (((0,), (0,)), ((), ())), precision=HIGH, preferred_element_type=F32
@@ -210,16 +218,16 @@
         g_x[it, b] = g_send[it, c]
         wait_gram = swap(4, it, block_peers, lambda j: g_send.at[it, lax.rem(j, nc)], g_x.at[it], b, nb - 1)
 
-        own_half = right_term(c)
-        half_copy.wait_recv()
-        q_sum[it] = (own_half + q_core[it]).reshape(q_sum.shape[1:])
-
-        def send_share(j, device):
-            @pl.when(j < owners)
-            def _():
-                remote(q_sum.at[it, j], q_x.at[it, chip], 5, it, device).start()
-
-        chip_peers(send_share)
+        for i, group in enumerate(groups):
+            own = right_term(c, group)
+            pieces[i].wait_recv()
+            q_sum[it, pl.ds(group * share, share)] = (own + q_core[it, i]).reshape(share, TILE, 128)
+            for k in range(share):
+                j = group * (nb // nc) + k
+
+                @pl.when(j != chip)
+                def _(j=j, k=k, group=group):
+                    remote(q_sum.at[it, group * share + k], q_x.at[it, chip], 5, it, (j * nc + c, y)).start()
 
         wait_gram()
         g_ag[it, c] = total(g_x.at[it], nb)
@@ -228,23 +236,23 @@
         gram_copy.start()
         pending.append(gram_copy.wait_send)
         remote(other_gram, other_gram, 6, it, partner).wait_recv()
-        pieces = []
+        blocks = []
         for h in range(nc):
             whole = g_ag[it, h]
-            pieces += [whole, pltpu.roll(whole, RANK, 1)]
+            blocks += [whole, pltpu.roll(whole, RANK, 1)]
         lane = lanes((RANK, 128))
         unit = (lane - RANK == lax.broadcasted_iota(jnp.int32, (RANK, 128), 0)).astype(F32)
-        eliminate(jnp.where(lane < RANK, jnp.concatenate(pieces, axis=0), unit), chol)
+        eliminate(jnp.where(lane < RANK, jnp.concatenate(blocks, axis=0), unit), chol)
         inverse = chol[...]
         turned = pltpu.roll(inverse, RANK, 1)
         solve = jnp.concatenate([jnp.where(lane < RANK, turned, 0.0), jnp.where(lane < RANK, 0.0, inverse)], axis=0)
 
-        @pl.when(chip < owners)
+        @pl.when(owns)
         def _():
-            q_x[it, chip] = q_sum[it, chip]
+            q_x[it, chip] = q_sum[it, mine_at]
             most = q_x.at[it, : chips - 1]
             remote(most, most, 5, it, partner).wait_recv()
-            mine = q_ag.at[it, c, chip]
+            mine = q_ag.at[it, c, mine_at]
             mine[...] = (nt(jnp.sum(q_x[it], axis=0), solve) / nrep).astype(BF16)
             chip_peers(lambda j, device: remote(mine, mine, 7, it, device).start())
 
@@ -269,12 +277,12 @@
             p_first, p_second = spread(left)
             p_first, p_second = p_first.astype(BF16), p_second.astype(BF16)
 
-        @pl.when(chip < owners)
+        @pl.when(owns)
         def _():
             others = q_ag.at[it, c, : owners - 1]
             remote(others, others, 7, it, partner).wait_recv()
 
-        @pl.when(chip >= owners)
+        @pl.when(jnp.logical_not(owns))
         def _():
             others = q_ag.at[it, c]
             remote(others, others, 7, it, partner).wait_recv()
@@ -287,31 +295,33 @@
         q_packed = q_ag[it].reshape(half, 128)
 
     q_turned = q_packed.T
-    right_ref[:, :half] = q_turned[:RANK]
-    right_ref[:, half:] = q_turned[RANK:]
-    stores = []
+    rv[:, :half] = q_turned[:RANK]
+    rv[:, half:] = q_turned[RANK:]
+    stores = [pltpu.make_async_copy(rv, right_out, store_sem.at[0])]
+    stores[0].start()
     for at_half, left_half in ((0, p_first), (half, p_second)):
-        span = slice(at_half, at_half + half)
+        span = pl.ds(at_half, half)
         rebuilt = jnp.dot(left_half, q_turned, preferred_element_type=F32)
         nev[:, span] = (gv[:, span].astype(F32) + ev[:, span].astype(F32) - rebuilt).astype(BF16)
-        stores.append(pltpu.make_async_copy(nev.at[:, span], ne_hbm.at[:, span], store_sem.at[len(stores)]))
+        stores.append(pltpu.make_async_copy(nev.at[:, span], ne_out.at[:, span], store_sem.at[len(stores)]))
         stores[-1].start()
 
     @pl.when(moved)
     def _():
         l_copy.wait()
 
-    left_ref[...] = l_recv[...]
+    stores.append(pltpu.make_async_copy(l_recv, left_out, store_sem.at[len(stores)]))
+    stores[-1].start()
     sized = size_ref.at[: chips - 1]
     for it in range(ITERS):
 
-        @pl.when(chip < owners)
+        @pl.when(owns)
         def _():
             most = q_sum.at[it, : owners - 1]
             remote(most, most, 5, it, partner).wait_send()
             remote(sized, sized, 7, it, partner).wait_send()
 
-        @pl.when(chip >= owners)
+        @pl.when(jnp.logical_not(owns))
         def _():
             remote(q_sum.at[it], q_sum.at[it], 5, it, partner).wait_send()
 
@@ -319,6 +329,15 @@
         done()
     for store in stores:
         store.wait()
+
+
+def place(*refs):
+    n = (len(refs) - 1) // 2
+    copies = [pltpu.make_async_copy(refs[i], refs[n + i], refs[-1].at[i]) for i in range(n)]
+    for copy in copies:
+        copy.start()
+    for copy in copies:
+        copy.wait()
 
 
 def step(geo, gradients, errors, warm_factor):
@@ -329,39 +348,50 @@
     half = cols // 2
     part = rows // 2 // ny
     core_rows = half // nc
+    piece = core_rows // nrep
     owners = core_rows // TILE
     stages = 10
     dma = pltpu.SemaphoreType.DMA
     vmem = pltpu.VMEM
     any_spec = pl.BlockSpec(memory_space=pl.ANY)
-    vmem_spec = pl.BlockSpec(memory_space=pltpu.VMEM)
-    return pl.pallas_call(
+    hbm_spec = pl.BlockSpec(memory_space=pltpu.HBM)
+    out_shape = (
+        jax.ShapeDtypeStruct((rows, cols), BF16),
+        jax.ShapeDtypeStruct((RANK, rows // nrep), F32),
+        jax.ShapeDtypeStruct((RANK, cols), BF16),
+    )
+    results = pl.pallas_call(
         functools.partial(kernel, geo),
-        out_shape=(
-            jax.ShapeDtypeStruct((rows, cols), BF16),
-            jax.ShapeDtypeStruct((RANK, rows // nrep), F32),
-            jax.ShapeDtypeStruct((RANK, cols), BF16),
-        ),
-        in_specs=[any_spec, any_spec, any_spec],
-        out_specs=(any_spec, vmem_spec, vmem_spec),
+        out_shape=out_shape,
+        in_specs=[hbm_spec] * 3,
+        out_specs=(any_spec,) * 3,
         scratch_shapes=[
             vmem((rows, cols), BF16), vmem((rows, cols), BF16), vmem((RANK, cols), BF16), vmem((rows, cols), BF16),
-            vmem((2, nc, core_rows, rows), BF16), vmem((rows, cols), BF16),
+            vmem((2, nc, nrep, piece, rows), BF16), vmem((rows, cols), BF16), vmem((RANK, cols), BF16),
             vmem((ITERS, ny, part, 128), F32), vmem((ITERS, ny, part, 128), F32),
             vmem((ITERS, nrep, part, 128), F32), vmem((ITERS, ny, part, 128), F32),
             vmem((ITERS, nc, TILE, 128), F32), vmem((ITERS, nb, TILE, 128), F32),
             vmem((ITERS, nc, TILE, 128), F32), vmem((RANK, 128), F32),
-            vmem((ITERS, core_rows, 128), F32), vmem((ITERS, core_rows, 128), F32),
+            vmem((ITERS, nrep, piece, 128), F32), vmem((ITERS, nrep, piece, 128), F32),
             vmem((ITERS, owners, TILE, 128), F32), vmem((ITERS, chips, TILE, 128), F32),
             vmem((ITERS, nc, owners, TILE, 128), BF16), vmem((chips, TILE, 128), BF16),
             vmem((nrep, RANK, rows // nrep), F32), vmem((RANK, rows // nrep), F32),
-            dma((3,)), dma((2,)), dma((stages, ITERS)), dma((stages, ITERS)),
+            dma((5,)), dma((4,)), dma((stages, ITERS)), dma((stages, ITERS)), dma((ITERS, nrep)), dma((ITERS, nrep)),
         ],
         compiler_params=pltpu.CompilerParams(
-            collective_id=0, has_side_effects=True, vmem_limit_bytes=60 * 1024 * 1024
+            collective_id=0, has_side_effects=True, vmem_limit_bytes=52 * 1024 * 1024
         ),
         name="power_step",
     )(gradients, errors, warm_factor)
+    return pl.pallas_call(
+        place,
+        out_shape=out_shape,
+        in_specs=[any_spec] * 3,
+        out_specs=(any_spec,) * 3,
+        scratch_shapes=[dma((3,))],
+        compiler_params=pltpu.CompilerParams(vmem_limit_bytes=8 * 1024 * 1024),
+        name="place",
+    )(*results)
 
 
 def build(mesh, geo):

time: 88.4 us -> 84.7 us (0.958)
  local copies, waits for them, and re-layouts: 3.51 us -> 0.93 us
  Pallas kernels: 84.1 us -> 82.9 us
    unnamed x7 -> x2, local copies, waits for them, and re-layouts: 3.51 us -> 0.93 us
    pallas_call x1 -> x2, Pallas kernels: 84.1 us -> 82.9 us  [the longest x1 81.9 us: step(): pl.pallas_call(functools.partial(kernel, geo), out_shape=out_shape, in_sp...]
where the time goes in v3:
time: 84.7 us; the launch traced here: 84.5 us
  Pallas kernels  82.9 us (98%)
  local copies, waits for them, and re-layouts  0.93 us (1%)
    pallas_call x1, Pallas kernels, step(): pl.pallas_call(functools.partial(kernel, geo), out_shape=out_shape, in_sp...  81.9 us

profile of v3, /device:TPU:1, one launch (start us, length us, event | category | flops | bytes accessed | tf_op | source)
XLA Modules:
  0.0 84.5 jit_solution(11414594502219808610)
XLA Ops:
  0.6 0.0 copy-start
  0.6 0.9 %copy-done = bf16[64,1792]{1,0:T(8,128)(2,1)S(1)} copy-done((bf16[64,1792]{1,0:T(8,128)(2,1)S(1)}, bf16[64,1792]{1,0:T(8,128)(2,1)}, u32[]{:S(2)}) %copy-start) | copy-done | bytes 229400
  1.6 81.9 %power_step.1 = (bf16[256,1792]{1,0:T(8,128)(2,1)S(1)}, f32[64,64]{1,0:T(8,128)S(1)}, bf16[64,1792]{1,0:T(8,128)(2,1)S(1)}) custom-call(bf16[256,1792]{1,0:T(8,128)(2,1)} %g_hbm.1, bf16[256,1792]{1,0:T(8,128)(2,1)} %e_hbm.1, bf16[64,1792]{1,0:T(8,128)(2,1)S(1)} %copy-done), custom_call_target="tpu_custom_call" | custom-call | tf_op jit(solution)/shard_map/power_step/pallas_call | solution.py:363
  83.5 1.0 %place.1 = (bf16[256,1792]{1,0:T(8,128)(2,1)}, f32[64,64]{1,0:T(8,128)}, bf16[64,1792]{1,0:T(8,128)(2,1)}) custom-call(bf16[256,1792]{1,0:T(8,128)(2,1)S(1)} %get-tuple-element.6.refs_0_, f32[64,64]{1,0:T(8,128)S(1)} %get-tuple-element.7.refs_1_, bf16[64,1792]{1,0:T(8,128)(2,1)S(1)} %get-tuple-element.8.refs_2_), custom_call_target="tpu_custom_call" | custom-call | tf_op jit(solution)/shard_map/place/pallas_call | solution.py:386
Async XLA Ops:
  0.6 0.9 %copy-start = (bf16[64,1792]{1,0:T(8,128)(2,1)S(1)}, bf16[64,1792]{1,0:T(8,128)(2,1)}, u32[]{:S(2)}) copy-start(bf16[64,1792]{1,0:T(8,128)(2,1)} %w_hbm.1) | copy-start | bytes 688132

commit v4 on v3

--- a/solution.py
+++ b/solution.py
@@ -59,7 +59,7 @@
 def kernel(
     geo, g_hbm, e_hbm, w_hbm, ne_out, left_out, right_out,
     gv, ev, wv, cv, ctv, nev, rv,
-    p_send, p_rs, p_z, p_ag, g_send, g_x, g_ag, chol,
+    p_send, p_rs, p_own, p_far, p_near, p_n, g_send, g_x, g_ag, chol,
     q_send, q_core, q_sum, q_x, q_ag, size_ref, l_send, l_recv,
     load_sem, store_sem, send_sem, recv_sem, piece_send, piece_recv,
 ):
@@ -83,7 +83,6 @@
     half_rows, half = rows // 2, cols // 2
     partner = (dp + 1 - 2 * c, y)
     l_dst = nrep * b + rep
-    l_src = lax.rem(dp, nrep) * nb + lax.div(dp, nrep)
     moved = l_dst != dp
 
     parts = [pl.ds(h * half_rows, half_rows) for h in range(2)]
@@ -97,10 +96,14 @@
             j = lax.rem(y + k, ny)
             act(j, (dp, j))
 
-    def rep_peers(act):
-        for k in sorted(range(1, nrep), key=lambda k: -min(k, nrep - k)):
-            j = lax.rem(rep + k, nrep)
-            act(j, (j * nb + b, y))
+    def far_peers(act):
+        far = lax.rem(rep + nrep // 2, nrep) * nb + b
+        for k in sorted(range(ny), key=lambda k: -min(k, ny - k)):
+            j = lax.rem(y + k, ny)
+            act(j, (far, j))
+
+    def near_device(step):
+        return (lax.rem(rep + nrep + step, nrep) * nb + b, y)
 
     def block_peers(act):
         for k in range(1, nb):
@@ -126,17 +129,11 @@
     def greet(device):
         pl.semaphore_signal(barrier, inc=1, device_id=device, device_id_type=MESH)
 
-    chip_peers(lambda j, device: greet(device))
     y_peers(lambda j, device: greet(device))
-    for k in range(nzl * nx):
-        greet((rep * nb + lax.rem(b + nc * k, nb) + 1 - 2 * c, y))
-
-    @pl.when(moved)
-    def _():
-        greet((l_dst, y))
-        greet((l_src, y))
-
-    greeted = chips - 1 + ny - 1 + nzl * nx
+    for k in range(1, nrep):
+        greet((lax.rem(rep + k, nrep) * nb + b, y))
+    block_peers(lambda j, device: greet(device))
+    greeted = ny - 1 + nrep - 1 + nb - 1
 
     def remote(src, dst, stage, it, device):
         return pltpu.make_async_remote_copy(
@@ -171,17 +168,27 @@
         packed = jnp.where(low, ones[0] + pltpu.roll(twos[0], RANK, 1), pltpu.roll(ones[1], RANK, 1) + twos[1])
         p_send[it] = packed.reshape(ny, half_rows // ny, 128)
         if it == 0:
-            pl.semaphore_wait(barrier, greeted + jnp.where(moved, 2, 0))
+            pl.semaphore_wait(barrier, greeted)
         wait = swap(0, it, y_peers, lambda j: p_send.at[it, j], p_rs.at[it], y, ny - 1)
         p_rs[it, y] = p_send[it, y]
         if it == 0:
             ctv[...] = cv[...].T.reshape(ctv.shape)
         wait()
-        p_z[it, rep] = total(p_rs.at[it], ny)
-        swap(1, it, rep_peers, lambda j: p_z.at[it, rep], p_z.at[it], rep, nrep - 1)()
-        p_ag[it, y] = total(p_z.at[it], nrep)
-        swap(2, it, y_peers, lambda j: p_ag.at[it, y], p_ag.at[it], y, ny - 1)()
-        p_whole = p_ag[it].reshape(half_rows, 128)
+        mine = p_own.at[it, y]
+        mine[...] = total(p_rs.at[it], ny)
+        for slot, step in ((1, 1), (0, -1)):
+            remote(mine, p_near.at[it, slot], 1, it, near_device(step)).start()
+        both = remote(p_near.at[it], p_near.at[it], 1, it, partner)
+        pending.append(both.wait_send)
+        wait_far = swap(2, it, far_peers, lambda j: mine, p_far.at[it], y, ny)
+        wait_own = swap(3, it, y_peers, lambda j: mine, p_own.at[it], y, ny - 1)
+        both.wait_recv()
+        p_n[it, y] = p_near[it, 0] + p_near[it, 1]
+        wait_near = swap(9, it, y_peers, lambda j: p_n.at[it, y], p_n.at[it], y, ny - 1)
+        wait_own()
+        wait_far()
+        wait_near()
+        p_whole = ((p_own[it] + p_far[it]) + p_n[it]).reshape(half_rows, 128)
 
         first, second = spread(p_whole)
         terms = list(zip(split2(first), split2(second)))
@@ -264,7 +271,7 @@
             for r in range(nrep):
                 h, o = r // per_half, r % per_half * wide
                 l_send[r] = turned_left[h * RANK : (h + 1) * RANK, o : o + wide]
-            l_copy = remote(l_send.at[rep], l_recv, 9, 0, (l_dst, y))
+            l_copy = remote(l_send.at[rep], l_recv, 10, 0, (l_dst, y))
 
             @pl.when(moved)
             def _():
@@ -350,7 +357,7 @@
     core_rows = half // nc
     piece = core_rows // nrep
     owners = core_rows // TILE
-    stages = 10
+    stages = 11
     dma = pltpu.SemaphoreType.DMA
     vmem = pltpu.VMEM
     any_spec = pl.BlockSpec(memory_space=pl.ANY)
@@ -369,7 +376,8 @@
             vmem((rows, cols), BF16), vmem((rows, cols), BF16), vmem((RANK, cols), BF16), vmem((rows, cols), BF16),
             vmem((2, nc, nrep, piece, rows), BF16), vmem((rows, cols), BF16), vmem((RANK, cols), BF16),
             vmem((ITERS, ny, part, 128), F32), vmem((ITERS, ny, part, 128), F32),
-            vmem((ITERS, nrep, part, 128), F32), vmem((ITERS, ny, part, 128), F32),
+            vmem((ITERS, ny, part, 128), F32), vmem((ITERS, ny, part, 128), F32),
+            vmem((ITERS, 2, part, 128), F32), vmem((ITERS, ny, part, 128), F32),
             vmem((ITERS, nc, TILE, 128), F32), vmem((ITERS, nb, TILE, 128), F32),
             vmem((ITERS, nc, TILE, 128), F32), vmem((RANK, 128), F32),
             vmem((ITERS, nrep, piece, 128), F32), vmem((ITERS, nrep, piece, 128), F32),

time: 84.7 us -> 82.2 us (0.970)
  Pallas kernels: 82.9 us -> 80.5 us
    pallas_call x1, Pallas kernels: 81.9 us -> 79.5 us  [step(): pl.pallas_call(functools.partial(kernel, geo), out_shape=out_shape, in_sp...]
where the time goes in v4:
time: 82.2 us; the launch traced here: 82.1 us
  Pallas kernels  80.5 us (98%)
  local copies, waits for them, and re-layouts  0.93 us (1%)
    pallas_call x1, Pallas kernels, step(): pl.pallas_call(functools.partial(kernel, geo), out_shape=out_shape, in_sp...  79.5 us

profile of v4, /device:TPU:1, one launch (start us, length us, event | category | flops | bytes accessed | tf_op | source)
XLA Modules:
  0.0 82.1 jit_solution(16760324212311134669)
XLA Ops:
  0.6 0.0 copy-start
  0.6 0.9 %copy-done = bf16[64,1792]{1,0:T(8,128)(2,1)S(1)} copy-done((bf16[64,1792]{1,0:T(8,128)(2,1)S(1)}, bf16[64,1792]{1,0:T(8,128)(2,1)}, u32[]{:S(2)}) %copy-start) | copy-done | bytes 229400
  1.6 79.5 %power_step.1 = (bf16[256,1792]{1,0:T(8,128)(2,1)S(1)}, f32[64,64]{1,0:T(8,128)S(1)}, bf16[64,1792]{1,0:T(8,128)(2,1)S(1)}) custom-call(bf16[256,1792]{1,0:T(8,128)(2,1)} %g_hbm.1, bf16[256,1792]{1,0:T(8,128)(2,1)} %e_hbm.1, bf16[64,1792]{1,0:T(8,128)(2,1)S(1)} %copy-done), custom_call_target="tpu_custom_call" | custom-call | tf_op jit(solution)/shard_map/power_step/pallas_call | solution.py:370
  81.0 1.0 %place.1 = (bf16[256,1792]{1,0:T(8,128)(2,1)}, f32[64,64]{1,0:T(8,128)}, bf16[64,1792]{1,0:T(8,128)(2,1)}) custom-call(bf16[256,1792]{1,0:T(8,128)(2,1)S(1)} %get-tuple-element.6.refs_0_, f32[64,64]{1,0:T(8,128)S(1)} %get-tuple-element.7.refs_1_, bf16[64,1792]{1,0:T(8,128)(2,1)S(1)} %get-tuple-element.8.refs_2_), custom_call_target="tpu_custom_call" | custom-call | tf_op jit(solution)/shard_map/place/pallas_call | solution.py:394
Async XLA Ops:
  0.6 0.9 %copy-start = (bf16[64,1792]{1,0:T(8,128)(2,1)S(1)}, bf16[64,1792]{1,0:T(8,128)(2,1)}, u32[]{:S(2)}) copy-start(bf16[64,1792]{1,0:T(8,128)(2,1)} %w_hbm.1) | copy-start | bytes 688132

commit v5 on v4

--- a/solution.py
+++ b/solution.py
@@ -34,8 +34,20 @@
     return hi, (x - hi.astype(F32)).astype(BF16)
 
 
-def nt(a, b):
-    return lax.dot_general(a, b, (((1,), (1,)), ((), ())), precision=HIGH, preferred_element_type=F32)
+def split3(x):
+    hi, rest = split2(x)
+    mid = rest
+    return hi, mid, (x - hi.astype(F32) - mid.astype(F32)).astype(BF16)
+
+
+def six_left(x):
+    hi, mid, lo = split3(x)
+    return jnp.concatenate([hi, hi, mid, hi, lo, mid], axis=1)
+
+
+def six_right(x):
+    hi, mid, lo = split3(x)
+    return jnp.concatenate([hi, mid, hi, lo, hi, mid], axis=0)
 
 
 def eliminate(rows, out_ref):
@@ -57,12 +69,13 @@
 
 
 def kernel(
-    geo, g_hbm, e_hbm, w_hbm, ne_out, left_out, right_out,
-    gv, ev, wv, cv, ctv, nev, rv,
-    p_send, p_rs, p_own, p_far, p_near, p_n, g_send, g_x, g_ag, chol,
+    geo, g_hbm, e_hbm, w_hbm, ne0, ne1, ne2, ne3, ne4, ne5, left_out, right_out,
+    gv, ev, wv, cv, cs, ctv, nev, rv,
+    p_send, p_rs, p_own, p_far, p_near, p_n, g_send, g_x, g_ag, chol, solver,
     q_send, q_core, q_sum, q_x, q_ag, size_ref, l_send, l_recv,
     load_sem, store_sem, send_sem, recv_sem, piece_send, piece_recv,
 ):
+    ne_outs = (ne0, ne1, ne2, ne3, ne4, ne5)
     nrep, nzl, nx, nc, ny = geo
     nb = nzl * nx * nc
     nz = nrep * nzl
@@ -85,12 +98,6 @@
     l_dst = nrep * b + rep
     moved = l_dst != dp
 
-    parts = [pl.ds(h * half_rows, half_rows) for h in range(2)]
-    pairs = [(w_hbm, wv)] + [(src.at[part], dst.at[part]) for part in parts for src, dst in ((g_hbm, gv), (e_hbm, ev))]
-    loads = [pltpu.make_async_copy(src, dst, load_sem.at[i]) for i, (src, dst) in enumerate(pairs)]
-    for load in loads:
-        load.start()
-
     def y_peers(act):
         for k in sorted(range(1, ny), key=lambda k: -min(k, ny - k)):
             j = lax.rem(y + k, ny)
@@ -134,6 +141,11 @@
         greet((lax.rem(rep + k, nrep) * nb + b, y))
     block_peers(lambda j, device: greet(device))
     greeted = ny - 1 + nrep - 1 + nb - 1
+    parts = [pl.ds(h * (rows // 4), rows // 4) for h in range(4)]
+    pairs = [(w_hbm, wv)] + [(src.at[part], dst.at[part]) for part in parts for src, dst in ((g_hbm, gv), (e_hbm, ev))]
+    loads = [pltpu.make_async_copy(src, dst, load_sem.at[i]) for i, (src, dst) in enumerate(pairs)]
+    for load in loads:
+        load.start()
 
     def remote(src, dst, stage, it, device):
         return pltpu.make_async_remote_copy(
@@ -157,15 +169,34 @@
     low = lanes((half_rows, 128)) < RANK
 
     for it in range(ITERS):
-        ones, twos = [], []
-        for h, part in enumerate(parts):
-            if it == 0:
+        if it == 0:
+            ones, twos = [], []
+            for h, part in enumerate(parts):
                 loads[1 + 2 * h].wait()
                 loads[2 + 2 * h].wait()
                 cv[part] = (gv[part].astype(F32) + ev[part].astype(F32)).astype(BF16)
-            ones.append(jnp.dot(cv[part, :half], q_packed, preferred_element_type=F32))
-            twos.append(jnp.dot(cv[part, half:], q_packed, preferred_element_type=F32))
-        packed = jnp.where(low, ones[0] + pltpu.roll(twos[0], RANK, 1), pltpu.roll(ones[1], RANK, 1) + twos[1])
+                ones.append(jnp.dot(cv[part, :half], q_packed, preferred_element_type=F32))
+                twos.append(jnp.dot(cv[part, half:], q_packed, preferred_element_type=F32))
+            one, two = jnp.concatenate(ones, axis=0), jnp.concatenate(twos, axis=0)
+            packed = jnp.where(
+                low,
+                one[:half_rows] + pltpu.roll(two[:half_rows], RANK, 1),
+                pltpu.roll(one[half_rows:], RANK, 1) + two[half_rows:],
+            )
+            one, two = jnp.concatenate(ones, axis=0), jnp.concatenate(twos, axis=0)
+        else:
+            own_q = q_ag[it - 1, c].reshape(half // nc, 128)
+            one = jnp.dot(cs[0, c], own_q, preferred_element_type=F32)
+            two = jnp.dot(cs[1, c], own_q, preferred_element_type=F32)
+            wait_other()
+            other_q = q_ag[it - 1, 1 - c].reshape(half // nc, 128)
+            one += jnp.dot(cs[0, 1 - c], other_q, preferred_element_type=F32)
+            two += jnp.dot(cs[1, 1 - c], other_q, preferred_element_type=F32)
+        packed = jnp.where(
+            low,
+            one[:half_rows] + pltpu.roll(two[:half_rows], RANK, 1),
+            pltpu.roll(one[half_rows:], RANK, 1) + two[half_rows:],
+        )
         p_send[it] = packed.reshape(ny, half_rows // ny, 128)
         if it == 0:
             pl.semaphore_wait(barrier, greeted)
@@ -173,22 +204,22 @@
         p_rs[it, y] = p_send[it, y]
         if it == 0:
             ctv[...] = cv[...].T.reshape(ctv.shape)
+            for i in range(2 * nc):
+                cs[i // nc, i % nc] = cv[:, i * (half // nc) : (i + 1) * (half // nc)]
         wait()
-        mine = p_own.at[it, y]
+        mine = p_own.at[it]
         mine[...] = total(p_rs.at[it], ny)
         for slot, step in ((1, 1), (0, -1)):
             remote(mine, p_near.at[it, slot], 1, it, near_device(step)).start()
         both = remote(p_near.at[it], p_near.at[it], 1, it, partner)
         pending.append(both.wait_send)
         wait_far = swap(2, it, far_peers, lambda j: mine, p_far.at[it], y, ny)
-        wait_own = swap(3, it, y_peers, lambda j: mine, p_own.at[it], y, ny - 1)
         both.wait_recv()
-        p_n[it, y] = p_near[it, 0] + p_near[it, 1]
+        p_n[it, y] = p_own[it] + (p_near[it, 0] + p_near[it, 1])
         wait_near = swap(9, it, y_peers, lambda j: p_n.at[it, y], p_n.at[it], y, ny - 1)
-        wait_own()
         wait_far()
         wait_near()
-        p_whole = ((p_own[it] + p_far[it]) + p_n[it]).reshape(half_rows, 128)
+        p_whole = (p_far[it] + p_n[it]).reshape(half_rows, 128)
 
         first, second = spread(p_whole)
         terms = list(zip(split2(first), split2(second)))
@@ -253,6 +284,10 @@
         inverse = chol[...]
         turned = pltpu.roll(inverse, RANK, 1)
         solve = jnp.concatenate([jnp.where(lane < RANK, turned, 0.0), jnp.where(lane < RANK, 0.0, inverse)], axis=0)
+        solver[...] = six_right(solve.T)
+
+        def solved(x):
+            return jnp.dot(six_left(x), solver[...], preferred_element_type=F32)
 
         @pl.when(owns)
         def _():
@@ -260,11 +295,11 @@
             most = q_x.at[it, : chips - 1]
             remote(most, most, 5, it, partner).wait_recv()
             mine = q_ag.at[it, c, mine_at]
-            mine[...] = (nt(jnp.sum(q_x[it], axis=0), solve) / nrep).astype(BF16)
+            mine[...] = (solved(jnp.sum(q_x[it], axis=0)) / nrep).astype(BF16)
             chip_peers(lambda j, device: remote(mine, mine, 7, it, device).start())
 
         if it == ITERS - 1:
-            left = nt(p_whole, solve)
+            left = solved(p_whole)
             turned_left = left.T
             per_half = nrep // 2
             wide = rows // nrep
@@ -298,20 +333,25 @@
         all_copy.start()
         pending.append(all_copy.wait_send)
         other = q_ag.at[it, 1 - c]
-        remote(other, other, 8, it, partner).wait_recv()
-        q_packed = q_ag[it].reshape(half, 128)
-
-    q_turned = q_packed.T
+        wait_other = remote(other, other, 8, it, partner).wait_recv
+
+    wait_other()
+    q_turned = q_ag[ITERS - 1].reshape(half, 128).T
     rv[:, :half] = q_turned[:RANK]
     rv[:, half:] = q_turned[RANK:]
     stores = [pltpu.make_async_copy(rv, right_out, store_sem.at[0])]
     stores[0].start()
-    for at_half, left_half in ((0, p_first), (half, p_second)):
-        span = pl.ds(at_half, half)
+    per_half = len(ne_outs) // 2
+    at = 0
+    for h, left_half in enumerate((p_first, p_second)):
+        span = pl.ds(h * half, half)
         rebuilt = jnp.dot(left_half, q_turned, preferred_element_type=F32)
         nev[:, span] = (gv[:, span].astype(F32) + ev[:, span].astype(F32) - rebuilt).astype(BF16)
-        stores.append(pltpu.make_async_copy(nev.at[:, span], ne_out.at[:, span], store_sem.at[len(stores)]))
-        stores[-1].start()
+        for ne_out in ne_outs[h * per_half : (h + 1) * per_half]:
+            wide = ne_out.shape[1]
+            stores.append(pltpu.make_async_copy(nev.at[:, pl.ds(at, wide)], ne_out, store_sem.at[len(stores)]))
+            stores[-1].start()
+            at += wide
 
     @pl.when(moved)
     def _():
@@ -339,8 +379,13 @@
 
 
 def place(*refs):
-    n = (len(refs) - 1) // 2
-    copies = [pltpu.make_async_copy(refs[i], refs[n + i], refs[-1].at[i]) for i in range(n)]
+    *sources, new_errors, left, right, sem = refs
+    pieces, targets, at = sources[:-2], [], 0
+    for piece in pieces:
+        targets.append(new_errors.at[:, pl.ds(at, piece.shape[1])])
+        at += piece.shape[1]
+    targets += [left, right]
+    copies = [pltpu.make_async_copy(src, dst, sem.at[i]) for i, (src, dst) in enumerate(zip(sources, targets))]
     for copy in copies:
         copy.start()
     for copy in copies:
@@ -367,36 +412,38 @@
         jax.ShapeDtypeStruct((RANK, rows // nrep), F32),
         jax.ShapeDtypeStruct((RANK, cols), BF16),
     )
+    unit = half // 7
+    widths = (2 * unit, 2 * unit, 3 * unit) * 2
     results = pl.pallas_call(
         functools.partial(kernel, geo),
-        out_shape=out_shape,
+        out_shape=tuple(jax.ShapeDtypeStruct((rows, wide), BF16) for wide in widths) + out_shape[1:],
         in_specs=[hbm_spec] * 3,
-        out_specs=(any_spec,) * 3,
+        out_specs=(any_spec,) * 8,
         scratch_shapes=[
             vmem((rows, cols), BF16), vmem((rows, cols), BF16), vmem((RANK, cols), BF16), vmem((rows, cols), BF16),
-            vmem((2, nc, nrep, piece, rows), BF16), vmem((rows, cols), BF16), vmem((RANK, cols), BF16),
+            vmem((2, nc, rows, core_rows), BF16), vmem((2, nc, nrep, piece, rows), BF16), vmem((rows, cols), BF16), vmem((RANK, cols), BF16),
             vmem((ITERS, ny, part, 128), F32), vmem((ITERS, ny, part, 128), F32),
-            vmem((ITERS, ny, part, 128), F32), vmem((ITERS, ny, part, 128), F32),
+            vmem((ITERS, part, 128), F32), vmem((ITERS, ny, part, 128), F32),
             vmem((ITERS, 2, part, 128), F32), vmem((ITERS, ny, part, 128), F32),
             vmem((ITERS, nc, TILE, 128), F32), vmem((ITERS, nb, TILE, 128), F32),
-            vmem((ITERS, nc, TILE, 128), F32), vmem((RANK, 128), F32),
+            vmem((ITERS, nc, TILE, 128), F32), vmem((RANK, 128), F32), vmem((6 * 128, 128), BF16),
             vmem((ITERS, nrep, piece, 128), F32), vmem((ITERS, nrep, piece, 128), F32),
             vmem((ITERS, owners, TILE, 128), F32), vmem((ITERS, chips, TILE, 128), F32),
             vmem((ITERS, nc, owners, TILE, 128), BF16), vmem((chips, TILE, 128), BF16),
             vmem((nrep, RANK, rows // nrep), F32), vmem((RANK, rows // nrep), F32),
-            dma((5,)), dma((4,)), dma((stages, ITERS)), dma((stages, ITERS)), dma((ITERS, nrep)), dma((ITERS, nrep)),
+            dma((9,)), dma((8,)), dma((stages, ITERS)), dma((stages, ITERS)), dma((ITERS, nrep)), dma((ITERS, nrep)),
         ],
         compiler_params=pltpu.CompilerParams(
-            collective_id=0, has_side_effects=True, vmem_limit_bytes=52 * 1024 * 1024
+            collective_id=0, has_side_effects=True, vmem_limit_bytes=(52 * 1024 + 640) * 1024
         ),
         name="power_step",
     )(gradients, errors, warm_factor)
     return pl.pallas_call(
         place,
         out_shape=out_shape,
-        in_specs=[any_spec] * 3,
+        in_specs=[any_spec] * 8,
         out_specs=(any_spec,) * 3,
-        scratch_shapes=[dma((3,))],
+        scratch_shapes=[dma((8,))],
         compiler_params=pltpu.CompilerParams(vmem_limit_bytes=8 * 1024 * 1024),
         name="place",
     )(*results)

time: 82.2 us -> 81.3 us (0.989)
  local copies, waits for them, and re-layouts: 0.93 us -> 0 us
    unnamed x2 -> x0, local copies, waits for them, and re-layouts: 0.93 us -> none
where the time goes in v5:
time: 81.3 us; the launch traced here: 81.1 us
  Pallas kernels  80.5 us (99%)
    pallas_call x1, Pallas kernels, step(): pl.pallas_call(functools.partial(kernel, geo), out_shape=tuple((jax.Shape...  79.4 us

profile of v5, /device:TPU:1, one launch (start us, length us, event | category | flops | bytes accessed | tf_op | source)
XLA Modules:
  0.0 81.1 jit_solution(12665190219646235453)
XLA Ops:
  0.6 79.4 %power_step.1 = (bf16[256,256]{1,0:T(8,128)(2,1)S(1)}, bf16[256,256]{1,0:T(8,128)(2,1)S(1)}, bf16[256,384]{1,0:T(8,128)(2,1)S(1)}, bf16[256,256]{1,0:T(8,128)(2,...) custom-call(bf16[256,1792]{1,0:T(8,128)(2,1)} %g_hbm.1, ...), custom_call_target="tpu_custom_call" | custom-call | tf_op jit(solution)/shard_map/power_step/pallas_call | solution.py:417
  80.0 1.1 %place.1 = (bf16[256,1792]{1,0:T(8,128)(2,1)}, f32[64,64]{1,0:T(8,128)}, bf16[64,1792]{1,0:T(8,128)(2,1)}) custom-call(bf16[256,256]{1,0:T(8,128)(2,1)S(1)} %get-tuple-element.11.refs_0_, bf16[256,256]{1,0:T(8,128)(2,1)S(1)} %get-tuple-element.12.refs_1_, bf16[256,384]{1,0:T(8,128)(2,1)S(1)} %get-tuple-element.13.refs_2_, ...), custom_call_target="tpu_custom_call" | custom-call | tf_op jit(solution)/shard_map/place/pallas_call | solution.py:441

commit v6 on v5

--- a/solution.py
+++ b/solution.py
@@ -51,26 +51,26 @@
 
 
 def eliminate(rows, out_ref):
-    block = 8
+    block = 16
     for k0 in range(0, RANK, block):
         n = rows.shape[0]
         cols = [jnp.broadcast_to(rows[:, k0 + j : k0 + j + 1], (n, 128)) for j in range(block)]
         for i in range(block):
-            pivot = cols[i][i : i + 1, :]
-            row = rows[i : i + 1, :]
-            out_ref[k0 + i : k0 + i + 1, :] = row * lax.rsqrt(pivot)
+            scale = lax.rsqrt(cols[i][i : i + 1, :])
+            row = rows[i : i + 1, :] * scale
+            out_ref[k0 + i : k0 + i + 1, :] = row
             if k0 + i == RANK - 1:
                 break
-            factor = cols[i] * (1.0 / pivot)
+            factor = cols[i] * scale
             rows = rows - factor * row
             for j in range(i + 1, block):
-                cols[j] = cols[j] - factor * cols[j][i : i + 1, :]
+                cols[j] = cols[j] - factor * (cols[j][i : i + 1, :] * scale)
         rows = rows[block:, :] if n > block else rows
 
 
 def kernel(
     geo, g_hbm, e_hbm, w_hbm, ne0, ne1, ne2, ne3, ne4, ne5, left_out, right_out,
-    gv, ev, wv, cv, cs, ctv, nev, rv,
+    gv, ev, wv, cv, cs, ctv, nev, rv, qt,
     p_send, p_rs, p_own, p_far, p_near, p_n, g_send, g_x, g_ag, chol, solver,
     q_send, q_core, q_sum, q_x, q_ag, size_ref, l_send, l_recv,
     load_sem, store_sem, send_sem, recv_sem, piece_send, piece_recv,
@@ -203,7 +203,10 @@
         wait = swap(0, it, y_peers, lambda j: p_send.at[it, j], p_rs.at[it], y, ny - 1)
         p_rs[it, y] = p_send[it, y]
         if it == 0:
-            ctv[...] = cv[...].T.reshape(ctv.shape)
+            turned_c = cv[...].T.reshape(2, nc, nrep, -1, rows)
+            for core in range(nc):
+                for group in range(nrep):
+                    ctv[core, group] = jnp.concatenate([turned_c[0, core, group], turned_c[1, core, group]], axis=1)
             for i in range(2 * nc):
                 cs[i // nc, i % nc] = cv[:, i * (half // nc) : (i + 1) * (half // nc)]
         wait()
@@ -222,15 +225,11 @@
         p_whole = (p_far[it] + p_n[it]).reshape(half_rows, 128)
 
         first, second = spread(p_whole)
-        terms = list(zip(split2(first), split2(second)))
+        parts_of_p = jnp.concatenate(split2(jnp.concatenate([first, second], axis=0)), axis=1)
 
         def right_term(core, group):
-            result = None
-            for one_p, two_p in terms:
-                term = jnp.dot(ctv[0, core, group], one_p, preferred_element_type=F32)
-                term += jnp.dot(ctv[1, core, group], two_p, preferred_element_type=F32)
-                result = term if result is None else result + term
-            return result
+            both = jnp.dot(ctv[core, group], parts_of_p, preferred_element_type=F32)
+            return both[:, :128] + both[:, 128:]
 
         groups = [lax.rem(rep + k, nrep) for k in sorted(range(nrep), key=lambda k: -min(k, nrep - k))]
         pieces = []
@@ -296,7 +295,18 @@
             remote(most, most, 5, it, partner).wait_recv()
             mine = q_ag.at[it, c, mine_at]
             mine[...] = (solved(jnp.sum(q_x[it], axis=0)) / nrep).astype(BF16)
-            chip_peers(lambda j, device: remote(mine, mine, 7, it, device).start())
+            for group in groups:
+                stage = 11 if group is groups[0] else 7
+                for k in range(nb // nc):
+                    j = group * (nb // nc) + k
+
+                    def send(j=j, stage=stage):
+                        remote(mine, mine, stage, it, (j * nc + c, y)).start()
+
+                    if group is groups[-1]:
+                        pl.when(j != chip)(send)
+                    else:
+                        send()
 
         if it == ITERS - 1:
             left = solved(p_whole)
@@ -319,34 +329,52 @@
             p_first, p_second = spread(left)
             p_first, p_second = p_first.astype(BF16), p_second.astype(BF16)
 
+        most = size_ref.at[: (nrep - 1) * share]
+
         @pl.when(owns)
         def _():
-            others = q_ag.at[it, c, : owners - 1]
+            others = size_ref.at[: (nrep - 1) * share - 1]
             remote(others, others, 7, it, partner).wait_recv()
 
         @pl.when(jnp.logical_not(owns))
         def _():
-            others = q_ag.at[it, c]
-            remote(others, others, 7, it, partner).wait_recv()
-
-        all_copy = remote(q_ag.at[it, c], q_ag.at[it, c], 8, it, partner)
-        all_copy.start()
-        pending.append(all_copy.wait_send)
-        other = q_ag.at[it, 1 - c]
-        wait_other = remote(other, other, 8, it, partner).wait_recv
-
+            remote(most, most, 7, it, partner).wait_recv()
+
+        for group in groups[1:] + groups[:1]:
+            slab = q_ag.at[it, c, pl.ds(group * share, share)]
+            passed = remote(slab, slab, 8, it, partner)
+            if group is groups[0]:
+                remote(slab, slab, 11, it, partner).wait_recv()
+            passed.start()
+        passed = remote(q_ag.at[it, c], q_ag.at[it, c], 8, it, partner)
+        pending.append(passed.wait_send)
+        wait_other = passed.wait_recv
+
+    early = half // nc // 128 * 128
+    late = half - early
+    halves = ((0, p_first), (half, p_second))
+
+    def renew(at, wide, q_part):
+        for start, left_half in halves:
+            span = pl.ds(pl.multiple_of(start + at, 128), wide)
+            rebuilt = jnp.dot(left_half, q_part, preferred_element_type=F32)
+            nev[:, span] = (gv[:, span].astype(F32) + ev[:, span].astype(F32) - rebuilt).astype(BF16)
+            yield
+
+    ahead = q_ag[ITERS - 1, c, pl.ds(c * ((late - half // nc) // TILE), early // TILE)]
+    for _ in renew(c * late, early, ahead.reshape(early, 128).T):
+        pass
     wait_other()
     q_turned = q_ag[ITERS - 1].reshape(half, 128).T
+    qt[...] = q_turned
     rv[:, :half] = q_turned[:RANK]
     rv[:, half:] = q_turned[RANK:]
     stores = [pltpu.make_async_copy(rv, right_out, store_sem.at[0])]
     stores[0].start()
     per_half = len(ne_outs) // 2
     at = 0
-    for h, left_half in enumerate((p_first, p_second)):
-        span = pl.ds(h * half, half)
-        rebuilt = jnp.dot(left_half, q_turned, preferred_element_type=F32)
-        nev[:, span] = (gv[:, span].astype(F32) + ev[:, span].astype(F32) - rebuilt).astype(BF16)
+    late_at = pl.multiple_of((1 - c) * early, 128)
+    for h, _ in enumerate(renew(late_at, late, qt[:, pl.ds(late_at, late)])):
         for ne_out in ne_outs[h * per_half : (h + 1) * per_half]:
             wide = ne_out.shape[1]
             stores.append(pltpu.make_async_copy(nev.at[:, pl.ds(at, wide)], ne_out, store_sem.at[len(stores)]))
@@ -359,7 +387,8 @@
 
     stores.append(pltpu.make_async_copy(l_recv, left_out, store_sem.at[len(stores)]))
     stores[-1].start()
-    sized = size_ref.at[: chips - 1]
+    sized = size_ref.at[: (nrep - 1) * (nb // nc) - 1]
+    far_sized = size_ref.at[: nb // nc]
     for it in range(ITERS):
 
         @pl.when(owns)
@@ -367,6 +396,7 @@
             most = q_sum.at[it, : owners - 1]
             remote(most, most, 5, it, partner).wait_send()
             remote(sized, sized, 7, it, partner).wait_send()
+            remote(far_sized, far_sized, 11, it, partner).wait_send()
 
         @pl.when(jnp.logical_not(owns))
         def _():
@@ -402,7 +432,7 @@
     core_rows = half // nc
     piece = core_rows // nrep
     owners = core_rows // TILE
-    stages = 11
+    stages = 12
     dma = pltpu.SemaphoreType.DMA
     vmem = pltpu.VMEM
     any_spec = pl.BlockSpec(memory_space=pl.ANY)
@@ -421,7 +451,7 @@
         out_specs=(any_spec,) * 8,
         scratch_shapes=[
             vmem((rows, cols), BF16), vmem((rows, cols), BF16), vmem((RANK, cols), BF16), vmem((rows, cols), BF16),
-            vmem((2, nc, rows, core_rows), BF16), vmem((2, nc, nrep, piece, rows), BF16), vmem((rows, cols), BF16), vmem((RANK, cols), BF16),
+            vmem((2, nc, rows, core_rows), BF16), vmem((nc, nrep, piece, 2 * rows), BF16), vmem((rows, cols), BF16), vmem((RANK, cols), BF16), vmem((128, half), BF16),
             vmem((ITERS, ny, part, 128), F32), vmem((ITERS, ny, part, 128), F32),
             vmem((ITERS, part, 128), F32), vmem((ITERS, ny, part, 128), F32),
             vmem((ITERS, 2, part, 128), F32), vmem((ITERS, ny, part, 128), F32),

time: 81.3 us -> 80.7 us (level)
  no operation moved by 1% of the time
where the time goes in v6:
time: 80.7 us; the launch traced here: 80.6 us
  Pallas kernels  79.9 us (99%)
    pallas_call x1, Pallas kernels, step(): pl.pallas_call(functools.partial(kernel, geo), out_shape=tuple((jax.Shape...  78.9 us

profile of v6, /device:TPU:1, one launch (start us, length us, event | category | flops | bytes accessed | tf_op | source)
XLA Modules:
  0.0 80.6 jit_solution(12306851540005711539)
XLA Ops:
  0.6 78.9 %power_step.1 = (bf16[256,256]{1,0:T(8,128)(2,1)S(1)}, bf16[256,256]{1,0:T(8,128)(2,1)S(1)}, bf16[256,384]{1,0:T(8,128)(2,1)S(1)}, bf16[256,256]{1,0:T(8,128)(2,...) custom-call(bf16[256,1792]{1,0:T(8,128)(2,1)} %g_hbm.1, ...), custom_call_target="tpu_custom_call" | custom-call | tf_op jit(solution)/shard_map/power_step/pallas_call | solution.py:447
  79.5 1.1 %place.1 = (bf16[256,1792]{1,0:T(8,128)(2,1)}, f32[64,64]{1,0:T(8,128)}, bf16[64,1792]{1,0:T(8,128)(2,1)}) custom-call(bf16[256,256]{1,0:T(8,128)(2,1)S(1)} %get-tuple-element.11.refs_0_, bf16[256,256]{1,0:T(8,128)(2,1)S(1)} %get-tuple-element.12.refs_1_, bf16[256,384]{1,0:T(8,128)(2,1)S(1)} %get-tuple-element.13.refs_2_, ...), custom_call_target="tpu_custom_call" | custom-call | tf_op jit(solution)/shard_map/place/pallas_call | solution.py:471

commit v7 on v6

--- a/solution.py
+++ b/solution.py
@@ -71,7 +71,7 @@
 def kernel(
     geo, g_hbm, e_hbm, w_hbm, ne0, ne1, ne2, ne3, ne4, ne5, left_out, right_out,
     gv, ev, wv, cv, cs, ctv, nev, rv, qt,
-    p_send, p_rs, p_own, p_far, p_near, p_n, g_send, g_x, g_ag, chol, solver,
+    p_send, p_rs, p_own, p_far, p_near, p_n, p_tie, p_some, g_send, g_x, g_ag, chol, solver,
     q_send, q_core, q_sum, q_x, q_ag, size_ref, l_send, l_recv,
     load_sem, store_sem, send_sem, recv_sem, piece_send, piece_recv,
 ):
@@ -200,25 +200,53 @@
         p_send[it] = packed.reshape(ny, half_rows // ny, 128)
         if it == 0:
             pl.semaphore_wait(barrier, greeted)
-        wait = swap(0, it, y_peers, lambda j: p_send.at[it, j], p_rs.at[it], y, ny - 1)
-        p_rs[it, y] = p_send[it, y]
+        tie_y = lax.rem(y + ny // 2, ny)
+        mine = p_own.at[it]
+        both = remote(p_near.at[it], p_near.at[it], 1, it, partner)
         if it == 0:
+            wait = swap(0, it, y_peers, lambda j: p_send.at[it, j], p_rs.at[it], y, ny - 1)
+            p_rs[it, y] = p_send[it, y]
             turned_c = cv[...].T.reshape(2, nc, nrep, -1, rows)
             for core in range(nc):
                 for group in range(nrep):
                     ctv[core, group] = jnp.concatenate([turned_c[0, core, group], turned_c[1, core, group]], axis=1)
             for i in range(2 * nc):
                 cs[i // nc, i % nc] = cv[:, i * (half // nc) : (i + 1) * (half // nc)]
-        wait()
-        mine = p_own.at[it]
-        mine[...] = total(p_rs.at[it], ny)
-        for slot, step in ((1, 1), (0, -1)):
-            remote(mine, p_near.at[it, slot], 1, it, near_device(step)).start()
-        both = remote(p_near.at[it], p_near.at[it], 1, it, partner)
+            wait()
+            mine[...] = total(p_rs.at[it], ny)
+            for slot, step in ((1, 1), (0, -1)):
+                remote(mine, p_near.at[it, slot], 1, it, near_device(step)).start()
+        else:
+            own_tie = remote(p_send.at[it, tie_y], p_tie.at[0], 3, it, (dp, tie_y))
+            own_tie.start()
+            for k in sorted(range(1, ny), key=lambda k: -min(k, ny - k)):
+                if k != ny // 2:
+                    j = lax.rem(y + k, ny)
+                    remote(p_send.at[it, j], p_rs.at[it, y], 0, it, (dp, j)).start()
+            for slot, step in ((2, 1), (1, -1)):
+                to = lax.rem(rep + nrep + step, nrep) * nb + b
+                remote(p_send.at[it, tie_y], p_tie.at[slot], 12, it, (to, tie_y)).start()
+            rest = remote(p_rs.at[it, : ny - 2], p_rs.at[it, : ny - 2], 0, it, partner)
+            near_ties = remote(p_tie.at[1:3], p_tie.at[1:3], 12, it, partner)
+            pending.extend([rest.wait_send, own_tie.wait_send, near_ties.wait_send])
+            rest.wait_recv()
+            some = p_send[it, y]
+            for k in range(1, ny):
+                if k != ny // 2:
+                    some = some + p_rs[it, lax.rem(y + k, ny)]
+            p_some[...] = some
+            for slot, step in ((1, 1), (0, -1)):
+                remote(p_some, p_near.at[it, slot], 1, it, near_device(step)).start()
+            own_tie.wait_recv()
+            mine[...] = some + p_tie[0]
         pending.append(both.wait_send)
         wait_far = swap(2, it, far_peers, lambda j: mine, p_far.at[it], y, ny)
         both.wait_recv()
-        p_n[it, y] = p_own[it] + (p_near[it, 0] + p_near[it, 1])
+        near = p_near[it, 0] + p_near[it, 1]
+        if it > 0:
+            near_ties.wait_recv()
+            near = near + (p_tie[1] + p_tie[2])
+        p_n[it, y] = p_own[it] + near
         wait_near = swap(9, it, y_peers, lambda j: p_n.at[it, y], p_n.at[it], y, ny - 1)
         wait_far()
         wait_near()
@@ -432,7 +460,7 @@
     core_rows = half // nc
     piece = core_rows // nrep
     owners = core_rows // TILE
-    stages = 12
+    stages = 13
     dma = pltpu.SemaphoreType.DMA
     vmem = pltpu.VMEM
     any_spec = pl.BlockSpec(memory_space=pl.ANY)
@@ -455,6 +483,7 @@
             vmem((ITERS, ny, part, 128), F32), vmem((ITERS, ny, part, 128), F32),
             vmem((ITERS, part, 128), F32), vmem((ITERS, ny, part, 128), F32),
             vmem((ITERS, 2, part, 128), F32), vmem((ITERS, ny, part, 128), F32),
+            vmem((3, part, 128), F32), vmem((part, 128), F32),
             vmem((ITERS, nc, TILE, 128), F32), vmem((ITERS, nb, TILE, 128), F32),
             vmem((ITERS, nc, TILE, 128), F32), vmem((RANK, 128), F32), vmem((6 * 128, 128), BF16),
             vmem((ITERS, nrep, piece, 128), F32), vmem((ITERS, nrep, piece, 128), F32),

time: 80.7 us -> 80.7 us (level)
  no operation moved by 1% of the time
where the time goes in v7:
time: 80.7 us; the launch traced here: 80.5 us
  Pallas kernels  79.9 us (99%)
    pallas_call x1, Pallas kernels, step(): pl.pallas_call(functools.partial(kernel, geo), out_shape=tuple((jax.Shape...  78.8 us

profile of v7, /device:TPU:1, one launch (start us, length us, event | category | flops | bytes accessed | tf_op | source)
XLA Modules:
  0.0 80.5 jit_solution(15871815406030122466)
XLA Ops:
  0.6 78.8 %power_step.1 = (bf16[256,256]{1,0:T(8,128)(2,1)S(1)}, bf16[256,256]{1,0:T(8,128)(2,1)S(1)}, bf16[256,384]{1,0:T(8,128)(2,1)S(1)}, bf16[256,256]{1,0:T(8,128)(2,...) custom-call(bf16[256,1792]{1,0:T(8,128)(2,1)} %g_hbm.1, ...), custom_call_target="tpu_custom_call" | custom-call | tf_op jit(solution)/shard_map/power_step/pallas_call | solution.py:475
  79.5 1.1 %place.1 = (bf16[256,1792]{1,0:T(8,128)(2,1)}, f32[64,64]{1,0:T(8,128)}, bf16[64,1792]{1,0:T(8,128)(2,1)}) custom-call(bf16[256,256]{1,0:T(8,128)(2,1)S(1)} %get-tuple-element.11.refs_0_, bf16[256,256]{1,0:T(8,128)(2,1)S(1)} %get-tuple-element.12.refs_1_, bf16[256,384]{1,0:T(8,128)(2,1)S(1)} %get-tuple-element.13.refs_2_, ...), custom_call_target="tpu_custom_call" | custom-call | tf_op jit(solution)/shard_map/place/pallas_call | solution.py:500
